TPU v7x, 128 devices: a whole 4x4x4 slice. The times are simulated.
128 devices in a mesh: wide: 64 (over y, x, z_hi, core), narrow: 2 (over z_lo).
Axes of the slice: x: 4, y: 4, z: 4 (z_hi: 2, z_lo: 2; z = z_hi * 2 + z_lo), core: 2. Of those that a mesh axis runs over, the one named last changes fastest.
Arguments:
- tokens: bfloat16 [16384, 1536], P('wide'), may hold values from -6 to 6
- doc_lengths: int32 [64, 4], P('wide'), may hold values from 1 to 128, 256 in all within a row
- norm_gain1: float32 [1536], replicated, may hold values from 0.5 to 1.5
- w_query: bfloat16 [1536, 1536], P('wide', 'narrow'), may hold values from -0.15625 to 0.15625
- b_query: float32 [1536], P('narrow'), may hold values from -3 to 3
- w_key: bfloat16 [1536, 256], P('wide', 'narrow'), may hold values from -0.15625 to 0.15625
- b_key: float32 [256], P('narrow'), may hold values from -3 to 3
- w_value: bfloat16 [1536, 256], P('wide', 'narrow'), may hold values from -0.15625 to 0.15625
- b_value: float32 [256], P('narrow'), may hold values from -3 to 3
- w_out: bfloat16 [1536, 1536], P('narrow', 'wide'), may hold values from -0.875 to 0.875
- norm_gain2: float32 [1536], replicated, may hold values from 0.5 to 1.5
- w_gate: bfloat16 [1536, 8960], P('wide', 'narrow'), may hold values from -0.15625 to 0.15625
- w_up: bfloat16 [1536, 8960], P('wide', 'narrow'), may hold values from -0.15625 to 0.15625
- w_down: bfloat16 [8960, 1536], P('narrow', 'wide'), may hold values from -0.0625 to 0.0625
- out_grad: bfloat16 [16384, 1536], P('wide'), may hold values from -16 to 16
Outputs:
- mixed_out: bfloat16 [16384, 1536], P('wide')
- grad_tokens: float32 [16384, 1536], P('wide')
- grad_gain1: float32 [1536], replicated
- grad_query: float32 [1536, 1536], P('wide', 'narrow')
- grad_qbias: float32 [1536], P('narrow')
- grad_key: float32 [1536, 256], P('wide', 'narrow')
- grad_kbias: float32 [256], P('narrow')
- grad_value: float32 [1536, 256], P('wide', 'narrow')
- grad_vbias: float32 [256], P('narrow')
- grad_outproj: float32 [1536, 1536], P('narrow', 'wide')
- grad_gain2: float32 [1536], replicated
- grad_gate: float32 [1536, 8960], P('wide', 'narrow')
- grad_up: float32 [1536, 8960], P('wide', 'narrow')
- grad_down: float32 [8960, 1536], P('narrow', 'wide')
Inputs may be any that keep to these rules, and one draw needn't show every extreme that they name: `doc_lengths`: each pack's 4 document lengths are positive and sum to 256; the longest is exactly 128.
All inputs are finite; a program needn't handle non-finite values.
Results may differ from a plain program's by a relative error of at most 0.022.
Values may be sent and summed in bfloat16 or wider, within the bound.
No kernel may reach another device: no remote copies, remote signals or barrier semaphores. Data moves between devices by JAX's collectives and lax.ppermute only.
A program may use at most 256 MiB of HBM per device.

v0:
```python
import jax
import jax.numpy as jnp
from jax import lax
from jax.sharding import PartitionSpec as P

HD = 128


rope_base = 10000.0
norm_eps = 1e-06


def contract_rows(left, right):
    return lax.dot_general(
        left, right, (((0,), (0,)), ((), ())), preferred_element_type=jnp.float32
    )


def contract_cols(left, right):
    return lax.dot_general(
        left, right, (((1,), (1,)), ((), ())), preferred_element_type=jnp.float32
    )


def rotate(value, cosine, sine):
    half = value.shape[-1] // 2
    first = value[..., :half]
    second = value[..., half:]
    return jnp.concatenate(
        [first * cosine - second * sine, second * cosine + first * sine], axis=-1
    )


def rotate_back(value, cosine, sine):
    half = value.shape[-1] // 2
    first = value[..., :half]
    second = value[..., half:]
    return jnp.concatenate(
        [first * cosine + second * sine, second * cosine - first * sine], axis=-1
    )


def doc_layout(lengths, count):
    ends = jnp.cumsum(lengths)
    starts = ends - lengths
    place = jnp.arange(count, dtype=jnp.int32)
    segment = jnp.sum((place[:, None] >= ends[None, :]).astype(jnp.int32), axis=1)
    labels = jnp.arange(lengths.shape[0], dtype=jnp.int32)
    first = jnp.sum(jnp.where(segment[:, None] == labels[None, :], starts[None, :], 0), axis=1)
    return (segment, place - first, place)


def on_device(
    tokens,
    doc_lengths,
    norm_gain1,
    w_query,
    b_query,
    w_key,
    b_key,
    w_value,
    b_value,
    w_out,
    norm_gain2,
    w_gate,
    w_up,
    w_down,
    out_grad,
):
    query_full, key_full, value_full, gate_full, up_full = (
        lax.all_gather(w_query, "wide", axis=0, tiled=True),
        lax.all_gather(w_key, "wide", axis=0, tiled=True),
        lax.all_gather(w_value, "wide", axis=0, tiled=True),
        lax.all_gather(w_gate, "wide", axis=0, tiled=True),
        lax.all_gather(w_up, "wide", axis=0, tiled=True),
    )
    out_full, down_full = (
        lax.all_gather(w_out, "wide", axis=1, tiled=True),
        lax.all_gather(w_down, "wide", axis=1, tiled=True),
    )
    rows = tokens.shape[0]
    local_heads = w_query.shape[1] // HD
    local_kv = w_key.shape[1] // HD
    group = local_heads // local_kv
    scale = HD ** (-0.5)
    segment, position, place = doc_layout(doc_lengths[0], rows)
    inverse = rope_base ** (-jnp.arange(0, HD, 2, dtype=jnp.float32) / HD)
    angle = position.astype(jnp.float32)[:, None] * inverse[None, :]
    cosine = jnp.cos(angle)[:, None, :]
    sine = jnp.sin(angle)[:, None, :]
    allowed = (segment[:, None] == segment[None, :]) & (place[None, :] <= place[:, None])
    inputs = tokens.astype(jnp.float32)
    factor_one = lax.rsqrt(jnp.mean(inputs * inputs, axis=-1, keepdims=True) + norm_eps)
    normed_one = inputs * factor_one
    h_one = (normed_one * norm_gain1).astype(jnp.bfloat16)
    q_lin = jnp.dot(h_one, query_full, preferred_element_type=jnp.float32) + b_query
    k_lin = jnp.dot(h_one, key_full, preferred_element_type=jnp.float32) + b_key
    v_lin = jnp.dot(h_one, value_full, preferred_element_type=jnp.float32) + b_value
    queries = (
        rotate(q_lin.reshape(rows, local_heads, HD), cosine, sine)
        .astype(jnp.bfloat16)
        .reshape(rows, local_kv, group, HD)
    )
    keys = rotate(k_lin.reshape(rows, local_kv, HD), cosine, sine).astype(jnp.bfloat16)
    values = v_lin.astype(jnp.bfloat16).reshape(rows, local_kv, HD)
    logits = jnp.einsum("ikgd,jkd->kgij", queries, keys, preferred_element_type=jnp.float32) * scale
    logits = jnp.where(allowed[None, None], logits, -1000000000.0)
    top = jnp.max(logits, axis=-1, keepdims=True)
    expo = jnp.exp(logits - top)
    probs = expo / jnp.sum(expo, axis=-1, keepdims=True)
    probs_low = probs.astype(jnp.bfloat16)
    attended = jnp.einsum("kgij,jkd->ikgd", probs_low, values, preferred_element_type=jnp.float32)
    attended = attended.reshape(rows, local_heads * HD).astype(jnp.bfloat16)
    resid = inputs + lax.psum(
        jnp.dot(attended, out_full, preferred_element_type=jnp.float32), "narrow"
    )
    factor_two = lax.rsqrt(jnp.mean(resid * resid, axis=-1, keepdims=True) + norm_eps)
    normed_two = resid * factor_two
    h_two = (normed_two * norm_gain2).astype(jnp.bfloat16)
    gate = jnp.dot(h_two, gate_full, preferred_element_type=jnp.float32)
    up_act = jnp.dot(h_two, up_full, preferred_element_type=jnp.float32)
    sigma = jax.nn.sigmoid(gate)
    swish = gate * sigma
    hidden = (swish * up_act).astype(jnp.bfloat16)
    mixed = resid + lax.psum(
        jnp.dot(hidden, down_full, preferred_element_type=jnp.float32).astype(jnp.bfloat16),
        "narrow",
    ).astype(jnp.float32)
    mixed_out = mixed.astype(jnp.bfloat16)
    grad_y = out_grad.astype(jnp.float32)
    d_down = contract_rows(hidden, out_grad)
    grad_hidden = contract_cols(out_grad, down_full)
    grad_gate_act = (grad_hidden * up_act * sigma * (1.0 + gate * (1.0 - sigma))).astype(
        jnp.bfloat16
    )
    grad_up_act = (grad_hidden * swish).astype(jnp.bfloat16)
    d_gate = contract_rows(h_two, grad_gate_act)
    d_up = contract_rows(h_two, grad_up_act)
    grad_h_two = lax.psum(
        (contract_cols(grad_gate_act, gate_full) + contract_cols(grad_up_act, up_full)).astype(
            jnp.bfloat16
        ),
        "narrow",
    ).astype(jnp.float32)
    gain_two_term = jnp.sum(grad_h_two * normed_two, axis=0)
    grad_n_two = grad_h_two * norm_gain2
    grad_resid = grad_y + factor_two * (
        grad_n_two - normed_two * jnp.mean(grad_n_two * normed_two, axis=-1, keepdims=True)
    )
    grad_branch = grad_resid.astype(jnp.bfloat16)
    d_out = contract_rows(attended, grad_branch)
    grad_att = (
        contract_cols(grad_branch, out_full).astype(jnp.bfloat16).reshape(rows, local_kv, group, HD)
    )
    grad_probs = jnp.einsum("ikgd,jkd->kgij", grad_att, values, preferred_element_type=jnp.float32)
    grad_vraw = jnp.einsum(
        "kgij,ikgd->jkd", probs_low, grad_att, preferred_element_type=jnp.float32
    )
    inner = jnp.sum(probs * grad_probs, axis=-1, keepdims=True)
    grad_logits = (probs * (grad_probs - inner)).astype(jnp.bfloat16)
    grad_qrot = (
        jnp.einsum("kgij,jkd->ikgd", grad_logits, keys, preferred_element_type=jnp.float32) * scale
    )
    grad_krot = (
        jnp.einsum("kgij,ikgd->jkd", grad_logits, queries, preferred_element_type=jnp.float32)
        * scale
    )
    grad_qlin = (
        rotate_back(grad_qrot.reshape(rows, local_heads, HD), cosine, sine)
        .reshape(rows, local_heads * HD)
        .astype(jnp.bfloat16)
    )
    grad_klin = (
        rotate_back(grad_krot, cosine, sine).reshape(rows, local_kv * HD).astype(jnp.bfloat16)
    )
    grad_vlin = grad_vraw.reshape(rows, local_kv * HD).astype(jnp.bfloat16)
    d_query = contract_rows(h_one, grad_qlin)
    d_key = contract_rows(h_one, grad_klin)
    d_value = contract_rows(h_one, grad_vlin)
    qbias_term = jnp.sum(grad_qlin.astype(jnp.float32), axis=0)
    kbias_term = jnp.sum(grad_klin.astype(jnp.float32), axis=0)
    vbias_term = jnp.sum(grad_vlin.astype(jnp.float32), axis=0)
    grad_h_one = lax.psum(
        (
            contract_cols(grad_qlin, query_full)
            + contract_cols(grad_klin, key_full)
            + contract_cols(grad_vlin, value_full)
        ).astype(jnp.bfloat16),
        "narrow",
    ).astype(jnp.float32)
    gain_one_term = jnp.sum(grad_h_one * normed_one, axis=0)
    grad_n_one = grad_h_one * norm_gain1
    grad_tokens = grad_resid + factor_one * (
        grad_n_one - normed_one * jnp.mean(grad_n_one * normed_one, axis=-1, keepdims=True)
    )
    grad_gain1, grad_gain2, grad_qbias, grad_kbias, grad_vbias = lax.psum(
        (gain_one_term, gain_two_term, qbias_term, kbias_term, vbias_term), "wide"
    )
    sum_query, sum_key, sum_value, sum_gate, sum_up = (
        lax.psum_scatter(d_query, "wide", scatter_dimension=0, tiled=True),
        lax.psum_scatter(d_key, "wide", scatter_dimension=0, tiled=True),
        lax.psum_scatter(d_value, "wide", scatter_dimension=0, tiled=True),
        lax.psum_scatter(d_gate, "wide", scatter_dimension=0, tiled=True),
        lax.psum_scatter(d_up, "wide", scatter_dimension=0, tiled=True),
    )
    sum_out, sum_down = (
        lax.psum_scatter(d_out, "wide", scatter_dimension=1, tiled=True),
        lax.psum_scatter(d_down, "wide", scatter_dimension=1, tiled=True),
    )
    return (
        mixed_out,
        grad_tokens,
        grad_gain1,
        sum_query,
        grad_qbias,
        sum_key,
        grad_kbias,
        sum_value,
        grad_vbias,
        sum_out,
        grad_gain2,
        sum_gate,
        sum_up,
        sum_down,
    )


def solution(mesh):
    placed = (
        P("wide", None),
        P("wide", None),
        P(),
        P("wide", "narrow"),
        P("narrow"),
        P("wide", "narrow"),
        P("narrow"),
        P("wide", "narrow"),
        P("narrow"),
        P("narrow", "wide"),
        P(),
        P("wide", "narrow"),
        P("wide", "narrow"),
        P("narrow", "wide"),
        P("wide", None),
    )
    return jax.shard_map(
        on_device,
        mesh=mesh,
        in_specs=placed,
        out_specs=(
            P("wide", None),
            P("wide", None),
            P(),
            P("wide", "narrow"),
            P("narrow"),
            P("wide", "narrow"),
            P("narrow"),
            P("wide", "narrow"),
            P("narrow"),
            P("narrow", "wide"),
            P(),
            P("wide", "narrow"),
            P("wide", "narrow"),
            P("narrow", "wide"),
        ),
        check_vma=False,
    )
```

profile of v0, /device:TPU:8, one launch (start us, length us, event | category | flops | bytes accessed | tf_op | source)
XLA Modules:
  0.0 2091.8 jit_solution(16559823227908687573)
XLA Ops:
  11.8 86.1 %all_gather.22 = bf16[1536,128]{1,0:T(8,128)(2,1)S(1)} all-gather(bf16[24,128]{1,0:T(8,128)(2,1)} %param.20), channel_id=1, replica_groups=mesh['wide'=64,'narrow'=2] {'wide'}, dimensions={0}, use_global_device_ids=true | all-gather | bytes 399360 | tf_op jit(solution)/shard_map/all_gather | solution.py:72
  99.8 87.3 %all_gather.21 = bf16[1536,128]{1,0:T(8,128)(2,1)S(1)} all-gather(bf16[24,128]{1,0:T(8,128)(2,1)S(1)} %copy-done.43), channel_id=1, replica_groups=mesh['wide'=64,'narrow'=2] {'wide'}, dimensions={0}, use_global_device_ids=true | all-gather | bytes 399360 | tf_op jit(solution)/shard_map/all_gather | solution.py:73
  191.1 2.5 convolution_add_fusion.3
  197.5 3.8 fusion.79
  203.3 67.5 %all-reduce.11.cloned.1.call-done = f32[256,1536]{1,0:T(8,128)} async-done(((f32[256,1536]{1,0:T(8,128)}), f32[256,1536]{1,0:T(8,128)}) %all-reduce.11.cloned.1.call-update) | async-done | bytes 1572880 | tf_op jit(solution)/shard_map/psum | solution.py:114
  273.3 99.2 %all-gather.12.cloned.1.call-done = bf16[1536,4480]{1,0:T(8,128)(2,1)} async-done(((bf16[24,4480]{1,0:T(8,128)(2,1)}), bf16[1536,4480]{1,0:T(8,128)(2,1)}) %all-gather.12.cloned.1.call-update) | async-done | bytes 13762576 | tf_op jit(solution)/shard_map/all_gather | solution.py:75
  372.5 10.4 fusion.81
  382.9 88.0 %all-gather.10.cloned.1.call-done = bf16[1536,4480]{1,0:T(8,128)(2,1)} async-done(((bf16[24,4480]{1,0:T(8,128)(2,1)}), bf16[1536,4480]{1,0:T(8,128)(2,1)}) %all-gather.10.cloned.1.call-update) | async-done | bytes 13762576 | tf_op jit(solution)/shard_map/all_gather | solution.py:74
  470.8 10.3 fusion.80
  481.2 88.0 %all-gather.14.cloned.1.call-done = bf16[4480,1536]{0,1:T(8,128)(2,1)} async-done(((bf16[4480,24]{0,1:T(8,128)(2,1)}), bf16[4480,1536]{0,1:T(8,128)(2,1)}) %all-gather.14.cloned.1.call-update) | async-done | bytes 13762576 | tf_op jit(solution)/shard_map/all_gather | solution.py:79
  569.2 14.0 multiply_convert_fusion
  583.2 8.7 fusion.82
  591.9 8.2 fusion.1
  600.4 10.4 convolution_convert_fusion
  610.8 28.3 %all-reduce.13.cloned.1.call-done = bf16[256,1536]{1,0:T(8,128)(2,1)} async-done(((bf16[256,1536]{1,0:T(8,128)(2,1)}), bf16[256,1536]{1,0:T(8,128)(2,1)}) %all-reduce.13.cloned.1.call-update) | async-done | bytes 786448 | tf_op jit(solution)/shard_map/psum | solution.py:139
  639.0 2.4 fusion.15
  647.1 3.3 convert_reduce_fusion.1
  656.6 2.5 fusion.83
  661.5 2.3 fusion.69
  666.1 4.4 fusion.36
  670.6 3.0 fusion.72
  674.0 14.9 fusion.86
  689.0 13.0 fusion.85
  702.0 13.0 fusion.84
  715.9 5.1 all-reduce.15.cloned.1.call-done
  722.9 288.8 %all-reduce.5 = (f32[1536]{0:T(1024)}, f32[768]{0:T(1024)}, f32[128]{0:T(128)}, f32[128]{0:T(128)}, f32[1536]{0:T(1024)}) all-reduce(f32[1536]{0:T(1024)S(1)} %get-tuple-element.16, f32[768]{0:T(1024)S(1)} %bitcast.139, f32[128]{0:T(128)S(1)} %convert_reduce_fusion.2, ...), channel_id=1, replica_groups=mesh['wide'=64,'narrow'=2] {'wide'}, use_global_device_ids=true, to_apply=%region_15.16 | all-reduce | flops 4096 | bytes 32768 | tf_op jit(solution)/shard_map/psum | solution.py:196
  1011.7 3.5 fusion.11
  1016.1 156.0 %reduce-scatter.20.cloned.1.call-done = f32[768,24]{0,1:T(8,128)} async-done(((f32[768,1536]{0,1:T(8,128)}), f32[768,24]{0,1:T(8,128)}) %reduce-scatter.20.cloned.1.call-update) | async-done | bytes 73744 | tf_op jit(solution)/shard_map/reduce_scatter | solution.py:207
  1172.1 155.8 %reduce-scatter.18.cloned.1.call-done = f32[24,768]{1,0:T(8,128)} async-done(((f32[1536,768]{1,0:T(8,128)}), f32[24,768]{1,0:T(8,128)}) %reduce-scatter.18.cloned.1.call-update) | async-done | bytes 73744 | tf_op jit(solution)/shard_map/reduce_scatter | solution.py:200
  1327.9 252.7 %reduce-scatter.30.cloned.1.call-done = f32[4480,24]{0,1:T(8,128)} async-done(((f32[4480,1536]{0,1:T(8,128)}), f32[4480,24]{0,1:T(8,128)}) %reduce-scatter.30.cloned.1.call-update) | async-done | bytes 430096
  1580.6 252.3 %reduce-scatter.28.cloned.1.call-done = f32[24,4480]{1,0:T(8,128)} async-done(((f32[1536,4480]{1,0:T(8,128)}), f32[24,4480]{1,0:T(8,128)}) %reduce-scatter.28.cloned.1.call-update) | async-done | bytes 430096
  1832.8 252.0 %reduce-scatter.26.cloned.1.call-done = f32[24,4480]{1,0:T(8,128)} async-done(((f32[1536,4480]{1,0:T(8,128)}), f32[24,4480]{1,0:T(8,128)}) %reduce-scatter.26.cloned.1.call-update) | async-done | bytes 430096
  (178 shorter events, 39.3 us)
Async XLA Ops:
  7.2 92.6 %copy-start.43 = (bf16[24,128]{1,0:T(8,128)(2,1)S(1)}, bf16[24,128]{1,0:T(8,128)(2,1)}, u32[]{:S(2)}) copy-start(bf16[24,128]{1,0:T(8,128)(2,1)} %param.22) | copy-start | bytes 18436
  7.2 183.9 %all-gather.6.cloned.1.call-start = ((), (), s32[]{:S(2)}) async-start(), calls=%async_computation.7 | async-start | bytes 2396160 | tf_op jit(solution)/shard_map/all_gather | solution.py:71
  7.9 189.6 %all-gather.8.cloned.1.call-start = ((), (), s32[]{:S(2)}) async-start(), calls=%async_computation.8 | async-start | bytes 2396160 | tf_op jit(solution)/shard_map/all_gather | solution.py:78
  8.7 262.1 %all-reduce.11.cloned.1.call-start = ((), (), s32[]{:S(2)}) async-start(), calls=%async_computation.9 | async-start | bytes 3145728 | tf_op jit(solution)/shard_map/psum | solution.py:114
  9.6 180.3 %copy-start.44 = (f32[64]{0:T(128)}, f32[64]{0:T(128)S(1)}, u32[]{:S(2)}) copy-start(f32[64]{0:T(128)S(1)} %multiply_power_fusion) | copy-start | bytes 772
  10.4 176.7 %copy-start = (bf16[256,1536]{1,0:T(8,128)(2,1)S(1)}, bf16[256,1536]{1,0:T(8,128)(2,1)}, u32[]{:S(2)}) copy-start(bf16[256,1536]{1,0:T(8,128)(2,1)} %param.15) | copy-start | bytes 2359300
  10.4 176.7 %copy-start.23 = (f32[1536]{0:T(1024)S(1)}, f32[1536]{0:T(1024)}, u32[]{:S(2)}) copy-start(f32[1536]{0:T(1024)} %param.17) | copy-start | bytes 18436
  10.4 176.7 %copy-start.48 = (f32[128]{0:T(128)S(1)}, f32[128]{0:T(128)}, u32[]{:S(2)}) copy-start(f32[128]{0:T(128)} %param.23) | copy-start | bytes 1540
  98.0 90.2 %copy-start.13 = (bf16[1536,128]{1,0:T(8,128)(2,1)}, bf16[1536,128]{1,0:T(8,128)(2,1)S(1)}, u32[]{:S(2)}) copy-start(bf16[1536,128]{1,0:T(8,128)(2,1)S(1)} %all_gather.22) | copy-start | bytes 1179652
  98.0 93.1 %copy-start.34 = (f32[256]{0:T(256)}, f32[256]{0:T(256)S(1)}, u32[]{:S(2)}) copy-start(f32[256]{0:T(256)S(1)} %add_rsqrt_fusion.1) | copy-start | bytes 3076
  99.8 91.3 %copy-start.47 = (f32[768]{0:T(1024)S(1)}, f32[768]{0:T(1024)}, u32[]{:S(2)}) copy-start(f32[768]{0:T(1024)} %param.19) | copy-start | bytes 9220
  187.1 4.0 copy-start.15
  197.5 3.8 copy-start.10
  201.3 171.2 %all-gather.12.cloned.1.call-start = ((), (), s32[]{:S(2)}) async-start(), calls=%async_computation.11 | async-start | bytes 13977600 | tf_op jit(solution)/shard_map/all_gather | solution.py:75
  201.9 269.0 %all-gather.10.cloned.1.call-start = ((), (), s32[]{:S(2)}) async-start(), calls=%async_computation.10 | async-start | bytes 13977600 | tf_op jit(solution)/shard_map/all_gather | solution.py:74
  202.5 366.7 %all-gather.14.cloned.1.call-start = ((), (), s32[]{:S(2)}) async-start(), calls=%async_computation.12 | async-start | bytes 13977600 | tf_op jit(solution)/shard_map/all_gather | solution.py:79
  203.1 70.0 %copy-start.31 = (f32[1536]{0:T(1024)S(1)}, f32[1536]{0:T(1024)}, u32[]{:S(2)}) copy-start(f32[1536]{0:T(1024)} %param.25) | copy-start | bytes 18436
  203.1 436.0 %all-reduce.13.cloned.1.call-start = ((), (), s32[]{:S(2)}) async-start(), calls=%async_computation.13 | async-start | bytes 1572864 | tf_op jit(solution)/shard_map/psum | solution.py:139
  583.2 8.7 copy-start.11
  583.2 8.7 copy-start.12
  600.2 120.8 %all-reduce.15.cloned.1.call-start = ((), (), s32[]{:S(2)}) async-start(), calls=%async_computation.21 | async-start | bytes 3145728 | tf_op jit(solution)/shard_map/psum | solution.py:125
  643.7 3.4 copy-start.33
  661.4 353.7 %reduce-scatter.24.cloned.1.call-start = ((), (), s32[]{:S(2)}) async-start(), calls=%async_computation.17 | async-start | bytes 798720
  663.8 352.3 %reduce-scatter.22.cloned.1.call-start = ((), (), s32[]{:S(2)}) async-start(), calls=%async_computation.16 | async-start | bytes 798720
  666.1 506.1 %reduce-scatter.20.cloned.1.call-start = ((), (), s32[]{:S(2)}) async-start(), calls=%async_computation.15 | async-start | bytes 4792320 | tf_op jit(solution)/shard_map/reduce_scatter | solution.py:207
  670.6 657.3 %reduce-scatter.18.cloned.1.call-start = ((), (), s32[]{:S(2)}) async-start(), calls=%async_computation.14 | async-start | bytes 4792320 | tf_op jit(solution)/shard_map/reduce_scatter | solution.py:200
  673.7 906.9 %reduce-scatter.30.cloned.1.call-start = ((), (), s32[]{:S(2)}) async-start(), calls=%async_computation.20 | async-start | bytes 27955200
  688.9 1143.9 %reduce-scatter.28.cloned.1.call-start = ((), (), s32[]{:S(2)}) async-start(), calls=%async_computation.19 | async-start | bytes 27955200
  702.0 1382.9 %reduce-scatter.26.cloned.1.call-start = ((), (), s32[]{:S(2)}) async-start(), calls=%async_computation.18 | async-start | bytes 27955200
  715.8 7.1 copy-start.38
  715.8 7.1 copy-start.46
  721.0 290.7 %copy-start.7 = (bf16[256,1536]{1,0:T(8,128)(2,1)S(1)}, bf16[256,1536]{1,0:T(8,128)(2,1)}, u32[]{:S(2)}) copy-start(bf16[256,1536]{1,0:T(8,128)(2,1)} %get-tuple-element.24) | copy-start | bytes 2359300
  (34 other events, 58.0 us)
Sparse Core Ops, SparseCore 0:
  11.1 69.9 all-gather.5
  84.2 65.8 all-gather.7
  201.4 69.3 all-reduce.10
  274.1 98.3 all-gather.11
  375.8 94.9 all-gather.9
  474.2 94.9 all-gather.13
  600.3 38.6 all-reduce.12
  661.6 59.3 all-reduce.14
  727.4 142.5 reduce-scatter.23
  876.1 139.9 reduce-scatter.21
  1022.9 149.1 reduce-scatter.19
  1178.7 149.1 reduce-scatter.17
  1335.8 244.7 reduce-scatter.29
  1588.3 244.4 reduce-scatter.27
  1840.6 244.2 reduce-scatter.25
where the time goes:
time: 2100 us; the launch traced here: 2090 us
  waiting for transfers between devices  1450 us (69%)
  blocking collectives  462 us (22%)
  matrix products  135 us (6%)
    unnamed x20, waiting for transfers between devices  761 us
    psum x1, blocking collectives, on_device(): lax.psum((gain_one_term, gain_two_term, qbias_term, kbias_term, vbias_ter...  289 us
    reduce_scatter x1, waiting for transfers between devices, on_device(): lax.psum_scatter(d_out, 'wide', scatter_dimension=1, tiled=True)  156 us
    reduce_scatter x1, waiting for transfers between devices, on_device(): lax.psum_scatter(d_query, 'wide', scatter_dimension=0, tiled=True)  156 us
    all_gather x1, waiting for transfers between devices, on_device(): lax.all_gather(w_up, 'wide', axis=0, tiled=True)  99.2 us
    all_gather x1, waiting for transfers between devices, on_device(): lax.all_gather(w_down, 'wide', axis=1, tiled=True)  88 us
    all_gather x1, waiting for transfers between devices, on_device(): lax.all_gather(w_gate, 'wide', axis=0, tiled=True)  88 us
    all_gather x1, blocking collectives, on_device(): lax.all_gather(w_value, 'wide', axis=0, tiled=True)  87.3 us
  transfers between devices with their start and end apart: 15, of which 12 were waited for; matrix products, arithmetic and copies ran while one was open for 5% of the time, Pallas kernels for 0%

commit v1 on v0

v1 whole, which is shorter than its diff:
```python
import jax
import jax.numpy as jnp
from jax import lax
from jax.sharding import Mesh, PartitionSpec as P

HD = 128
BF = jnp.bfloat16
F32 = jnp.float32
rope_base = 10000.0
norm_eps = 1e-06
WIDE = ("y", "x", "zh", "c")
EVERY = ("y", "x", "zh", "c", "zl")
SLICE = 1152


def mm(left, right):
    return jnp.dot(left, right, preferred_element_type=F32)


def contract_rows(left, right):
    return lax.dot_general(left, right, (((0,), (0,)), ((), ())), preferred_element_type=F32)


def contract_cols(left, right):
    return lax.dot_general(left, right, (((1,), (1,)), ((), ())), preferred_element_type=F32)


def hop(value, axis, step):
    size = lax.axis_size(axis)
    return lax.ppermute(value, axis, [(i, (i + step) % size) for i in range(size)])


def zhop(value, step):
    return lax.ppermute(value, ("zh", "zl"), [(i, (i + step) % 4) for i in range(4)])


def in_order(pieces, axis, me, dim):
    count = len(pieces)
    shape = list(pieces[0].shape)
    shape.insert(dim, count)
    whole = jnp.zeros(shape, pieces[0].dtype)
    for k, piece in enumerate(pieces):
        whole = lax.dynamic_update_index_in_dim(whole, piece, (me - k) % count, dim)
    return whole


def ring_pieces(value, axis):
    return [value, hop(value, axis, 1), hop(value, axis, 2), hop(value, axis, 3)]


def pair(mine, theirs, side, dim):
    first = jnp.where(side == 0, mine, theirs)
    second = jnp.where(side == 0, theirs, mine)
    return jnp.stack([first, second], dim)


def gather_rows(value, spot):
    y, x, zh, c = spot
    cols = value.shape[1]
    both = pair(value, hop(value, "zh", 1), zh, 0)
    half = cols // 2
    left, right = both[..., :half], both[..., half:]
    left = in_order(ring_pieces(left, "x"), "x", x, 0)
    right = in_order(ring_pieces(right, "y"), "y", y, 0)
    left = in_order(ring_pieces(left, "y"), "y", y, 0)
    right = in_order(ring_pieces(right, "x"), "x", x, 1)
    whole = jnp.concatenate([left, right], -1)
    other = hop(whole, "c", 1)
    return pair(whole, other, c, 3).reshape(1536, cols)


def trade(blocks, zh, c):
    me = zh * 2 + c
    got = []
    for k in range(4):
        block = lax.dynamic_index_in_dim(blocks, me ^ k, 0, keepdims=False)
        if k:
            block = lax.ppermute(block, ("zh", "c"), [(i, i ^ k) for i in range(4)])
        got.append(block)
    whole = jnp.zeros(blocks.shape, blocks.dtype)
    for k in range(4):
        whole = lax.dynamic_update_index_in_dim(whole, got[k], me ^ k, 0)
    return whole


def gather_tokens(value):
    ring = jnp.concatenate([value, zhop(value, 1), zhop(value, 3), zhop(value, 2)], 0)
    return jnp.concatenate([ring, hop(ring, "c", 1)], 0)


def sum_tokens(part):
    half = part.shape[0] // 2
    quarter = half // 4
    mine = part[:half].astype(F32) + hop(part[half:].astype(BF), "c", 1).astype(F32)
    sent = mine.astype(BF)
    back = zhop(sent[quarter : 2 * quarter], 3)
    ahead = zhop(sent[2 * quarter : 3 * quarter], 1)
    far = zhop(sent[3 * quarter :], 2)
    return mine[:quarter] + back.astype(F32) + ahead.astype(F32) + far.astype(F32)


def rotate(value, cosine, sine):
    half = value.shape[-1] // 2
    first = value[..., :half]
    second = value[..., half:]
    return jnp.concatenate(
        [first * cosine - second * sine, second * cosine + first * sine], axis=-1
    )


def doc_layout(lengths, count):
    ends = jnp.cumsum(lengths)
    starts = ends - lengths
    place = jnp.arange(count, dtype=jnp.int32)
    segment = jnp.sum((place[:, None] >= ends[None, :]).astype(jnp.int32), axis=1)
    labels = jnp.arange(lengths.shape[0], dtype=jnp.int32)
    first = jnp.sum(jnp.where(segment[:, None] == labels[None, :], starts[None, :], 0), axis=1)
    return (segment, place - first, place)


def own_rows(value, side):
    half = value.shape[0] // 2
    return lax.dynamic_slice_in_dim(value, side * half, half, 0)


def both_rows(mine, zl):
    return pair(mine, hop(mine, "zl", 1), zl, 0).reshape(2 * mine.shape[0], mine.shape[1])


def on_device(
    tokens,
    doc_lengths,
    norm_gain1,
    w_query,
    b_query,
    w_key,
    b_key,
    w_value,
    b_value,
    w_out,
    norm_gain2,
    w_gate,
    w_up,
    w_down,
    out_grad,
):
    y, x, zh, c, zl = (lax.axis_index(axis) for axis in EVERY)
    spot = (y, x, zh, c)
    rows = tokens.shape[0]
    hidden_units = w_gate.shape[1]
    pad = 4 * SLICE - hidden_units
    scale = HD ** (-0.5)

    qkv_full = gather_rows(jnp.concatenate([w_query, w_key, w_value], 1), spot)
    out_full = gather_rows(w_out.T, spot)
    ffn = jnp.stack([w_gate, w_up, w_down.T], 1)
    ffn = jnp.pad(ffn, ((0, 0), (0, 0), (0, pad))).reshape(24, 3, 4, SLICE)
    ffn = trade(ffn.transpose(2, 0, 1, 3).reshape(4, 24, 3 * SLICE), zh, c)
    ffn_full = lax.all_gather(ffn.reshape(96, 3 * SLICE), ("y", "x"), axis=0, tiled=True)
    gate_up_full, down_full = ffn_full[:, : 2 * SLICE], ffn_full[:, 2 * SLICE :]
    grad_all = gather_tokens(own_rows(out_grad, zl))

    local_heads = w_query.shape[1] // HD
    segment, position, place = doc_layout(doc_lengths[0], rows)
    inverse = rope_base ** (-jnp.arange(0, HD, 2, dtype=F32) / HD)
    angle = position.astype(F32)[:, None] * inverse[None, :]
    cosine = jnp.cos(angle)[:, None, :]
    sine = jnp.sin(angle)[:, None, :]
    allowed = (segment[:, None] == segment[None, :]) & (place[None, :] <= place[:, None])
    inputs = tokens.astype(F32)
    factor_one = lax.rsqrt(jnp.mean(inputs * inputs, axis=-1, keepdims=True) + norm_eps)
    normed_one = inputs * factor_one
    h_one = (normed_one * norm_gain1).astype(BF)
    qkv = mm(h_one, qkv_full) + jnp.concatenate([b_query, b_key, b_value])
    q_cols = local_heads * HD
    queries = rotate(qkv[:, :q_cols].reshape(rows, local_heads, HD), cosine, sine).astype(BF)
    keys = rotate(qkv[:, q_cols : q_cols + HD].reshape(rows, 1, HD), cosine, sine)
    keys = keys.astype(BF).reshape(rows, HD)
    values = qkv[:, q_cols + HD :].astype(BF)
    logits = jnp.einsum("igd,jd->gij", queries, keys, preferred_element_type=F32) * scale
    logits = jnp.where(allowed[None], logits, -1000000000.0)
    top = jnp.max(logits, axis=-1, keepdims=True)
    expo = jnp.exp(logits - top)
    probs = expo / jnp.sum(expo, axis=-1, keepdims=True)
    probs_low = probs.astype(BF)
    attended = jnp.einsum("gij,jd->igd", probs_low, values, preferred_element_type=F32)
    attended = attended.reshape(rows, q_cols).astype(BF)
    branch = contract_cols(attended, out_full)
    theirs = hop(own_rows(branch, 1 - zl).astype(BF), "zl", 1)
    resid = own_rows(tokens, zl).astype(F32) + own_rows(branch, zl) + theirs.astype(F32)

    factor_two = lax.rsqrt(jnp.mean(resid * resid, axis=-1, keepdims=True) + norm_eps)
    normed_two = resid * factor_two
    h_two = gather_tokens((normed_two * norm_gain2).astype(BF))
    gate_up = mm(h_two, gate_up_full)
    grad_hidden = mm(grad_all, down_full)
    gate, up_act = gate_up[:, :SLICE], gate_up[:, SLICE:]
    sigma = jax.nn.sigmoid(gate)
    swish = gate * sigma
    hidden = (swish * up_act).astype(BF)
    grad_gate_act = (grad_hidden * up_act * sigma * (1.0 + gate * (1.0 - sigma))).astype(BF)
    grad_up_act = (grad_hidden * swish).astype(BF)
    grad_act = jnp.concatenate([grad_gate_act, grad_up_act], 1)
    grad_h_two = sum_tokens(contract_cols(grad_act, gate_up_full))
    d_ffn = jnp.concatenate(
        [contract_rows(h_two, grad_act).astype(BF), contract_rows(grad_all, hidden).astype(BF)], 1
    )
    mixed = (resid + sum_tokens(contract_cols(hidden, down_full))).astype(BF)
    mixed_out = both_rows(mixed, zl)
    d_ffn = lax.psum_scatter(d_ffn, ("y", "x"), scatter_dimension=0, tiled=True)
    d_ffn = trade(d_ffn.reshape(4, 24, 3 * SLICE), zh, c).astype(F32)
    d_ffn = d_ffn.reshape(4, 24, 3, SLICE).transpose(2, 1, 0, 3).reshape(3, 24, 4 * SLICE)
    d_gate, d_up, d_down = (d_ffn[i, :, :hidden_units] for i in range(3))

    gain_two_term = jnp.sum(grad_h_two * normed_two, axis=0)
    grad_n_two = grad_h_two * norm_gain2
    grad_resid = own_rows(out_grad, zl).astype(F32) + factor_two * (
        grad_n_two - normed_two * jnp.mean(grad_n_two * normed_two, axis=-1, keepdims=True)
    )
    grad_branch = both_rows(grad_resid.astype(BF), zl)
    d_out = contract_rows(grad_branch, attended)
    grad_att = mm(grad_branch, out_full).astype(BF).reshape(rows, local_heads, HD)

    grad_probs = jnp.einsum("igd,jd->gij", grad_att, values, preferred_element_type=F32)
    grad_vraw = jnp.einsum("gij,igd->jd", probs_low, grad_att, preferred_element_type=F32)
    inner = jnp.sum(probs * grad_probs, axis=-1, keepdims=True)
    grad_logits = (probs * (grad_probs - inner)).astype(BF)
    grad_qrot = jnp.einsum("gij,jd->igd", grad_logits, keys, preferred_element_type=F32) * scale
    grad_krot = jnp.einsum("gij,igd->jd", grad_logits, queries, preferred_element_type=F32) * scale
    grad_qlin = rotate(grad_qrot, cosine, -sine).reshape(rows, q_cols).astype(BF)
    grad_klin = rotate(grad_krot[:, None, :], cosine, -sine).reshape(rows, HD).astype(BF)
    grad_qkv = jnp.concatenate([grad_qlin, grad_klin, grad_vraw.astype(BF)], 1)
    d_qkv = contract_rows(h_one, grad_qkv)
    bias_term = jnp.sum(grad_qkv.astype(F32), axis=0)

    grad_h_part = contract_cols(grad_qkv, qkv_full)
    theirs = hop(own_rows(grad_h_part, 1 - zl).astype(BF), "zl", 1)
    grad_h_one = own_rows(grad_h_part, zl) + theirs.astype(F32)
    my_normed = own_rows(normed_one, zl)
    gain_one_term = jnp.sum(grad_h_one * my_normed, axis=0)
    grad_n_one = grad_h_one * norm_gain1
    grad_tokens = grad_resid + own_rows(factor_one, zl) * (
        grad_n_one - my_normed * jnp.mean(grad_n_one * my_normed, axis=-1, keepdims=True)
    )
    grad_tokens = both_rows(grad_tokens.astype(BF), zl).astype(F32)

    d_attn = jnp.concatenate([d_qkv.astype(BF), d_out.astype(BF)], 1)
    d_attn = sum_rows(d_attn, spot)
    cols = qkv_full.shape[1]
    d_query, d_key, d_value, d_outproj = jnp.split(d_attn, [q_cols, q_cols + HD, cols], 1)
    gain_one, gain_two = lax.psum((gain_one_term, gain_two_term), EVERY)
    bias = lax.psum(bias_term, WIDE)
    d_qbias, d_kbias, d_vbias = jnp.split(bias, [q_cols, q_cols + HD])
    return (
        mixed_out,
        grad_tokens,
        gain_one,
        d_query,
        d_qbias,
        d_key,
        d_kbias,
        d_value,
        d_vbias,
        d_outproj.T,
        gain_two,
        d_gate,
        d_up,
        d_down.T,
    )


def ring_sum(value, axis, me, dim):
    def block(k):
        return lax.dynamic_index_in_dim(value, (me + k) % 4, dim, keepdims=False)

    total = block(0).astype(F32)
    for k in (1, 2, 3):
        total = total + hop(block(k), axis, k).astype(F32)
    return total


def sum_rows(value, spot):
    y, x, zh, c = spot
    cols = value.shape[1]
    value = value.reshape(4, 4, 2, 2, 24, cols)
    mine = lax.dynamic_index_in_dim(value, c, 3, keepdims=False)
    other = lax.dynamic_index_in_dim(value, 1 - c, 3, keepdims=False)
    value = (mine.astype(F32) + hop(other, "c", 1).astype(F32)).astype(BF)
    half = cols // 2
    left, right = value[..., :half], value[..., half:]
    left = ring_sum(left, "y", y, 0).astype(BF)
    right = ring_sum(right, "x", x, 1).astype(BF)
    left = ring_sum(left, "x", x, 0)
    right = ring_sum(right, "y", y, 0)
    both = jnp.concatenate([left, right], -1)
    mine = lax.dynamic_index_in_dim(both, zh, 0, keepdims=False)
    other = lax.dynamic_index_in_dim(both, 1 - zh, 0, keepdims=False)
    return mine + hop(other.astype(BF), "zh", 1).astype(F32)


def solution(mesh):
    split = Mesh(mesh.devices.reshape(4, 4, 2, 2, 2), EVERY)
    return jax.shard_map(
        on_device,
        mesh=split,
        in_specs=(
            P(WIDE, None),
            P(WIDE, None),
            P(),
            P(WIDE, "zl"),
            P("zl"),
            P(WIDE, "zl"),
            P("zl"),
            P(WIDE, "zl"),
            P("zl"),
            P("zl", WIDE),
            P(),
            P(WIDE, "zl"),
            P(WIDE, "zl"),
            P("zl", WIDE),
            P(WIDE, None),
        ),
        out_specs=(
            P(WIDE, None),
            P(WIDE, None),
            P(),
            P(WIDE, "zl"),
            P("zl"),
            P(WIDE, "zl"),
            P("zl"),
            P(WIDE, "zl"),
            P("zl"),
            P("zl", WIDE),
            P(),
            P(WIDE, "zl"),
            P(WIDE, "zl"),
            P("zl", WIDE),
        ),
        check_vma=False,
    )
```

time: 2100 us -> 699 us (0.33)
  waiting for transfers between devices: 1450 us -> 184 us
  blocking collectives: 462 us -> 230 us
  starting transfers between devices: 1.24 us -> 83.2 us
  matrix products: 135 us -> 72.3 us
  local copies, waits for them, and re-layouts: 8.88 us -> 54.8 us
  other arithmetic: 20.4 us -> 48.6 us
    unnamed x20 -> x2, waiting for transfers between devices: 761 us -> 0.03 us
    reduce_scatter x2 -> x1, waiting for transfers between devices: 312 us -> 0.01 us  [on_device(): d_ffn = lax.psum_scatter(d_ffn, ('y', 'x'), scatter_dimension=0, tiled=True)]
    all_gather x5 -> x1, waiting for transfers between devices: 275 us -> 0.01 us  [on_device(): lax.all_gather(ffn.reshape(96, 3 * SLICE), ('y', 'x'), axis=0, tiled=True)]
    ppermute x0 -> x69, waiting for transfers between devices: none -> 184 us  [the longest x51 138 us: hop(): lax.ppermute(value, axis, [(i, (i + step) % size) for i in range(size)])]
    all_gather x2 -> x0, blocking collectives: 173 us -> none  [the longest x1 87.3 us: on_device(): lax.all_gather(w_value, 'wide', axis=0, tiled=True)]
    psum x3 -> x0, waiting for transfers between devices: 101 us -> none  [the longest x1 67.5 us: on_device(): lax.psum(jnp.dot(attended, out_full, preferred_element_type=jnp.float32),...]
    ppermute x0 -> x69, starting transfers between devices: none -> 83.1 us  [the longest x51 56.1 us: hop(): lax.ppermute(value, axis, [(i, (i + step) % size) for i in range(size)])]
    psum x1 -> x2, blocking collectives: 289 us -> 230 us  [the longest x1 147 us: on_device(): bias = lax.psum(bias_term, WIDE)]
  transfers between devices with their start and end apart: 15 -> 71, of which waited for: 12 -> 33; matrix products, arithmetic and copies ran while one was open for 5% -> 17% of each run, Pallas kernels for 0% -> 0%
where the time goes in v1:
time: 699 us; the launch traced here: 689 us
  blocking collectives  230 us (33%)
  waiting for transfers between devices  184 us (26%)
  starting transfers between devices  83.2 us (12%)
  matrix products  72.3 us (10%)
  local copies, waits for them, and re-layouts  54.8 us (8%)
  other arithmetic  48.6 us (7%)
  between operations  16.1 us (2%)
    psum x1, blocking collectives, on_device(): bias = lax.psum(bias_term, WIDE)  147 us
    ppermute x51, waiting for transfers between devices, hop(): lax.ppermute(value, axis, [(i, (i + step) % size) for i in range(size)])  138 us
    psum x1, blocking collectives, on_device(): gain_one, gain_two = lax.psum((gain_one_term, gain_two_term), EVERY)  82.3 us
    ppermute x51, starting transfers between devices, hop(): lax.ppermute(value, axis, [(i, (i + step) % size) for i in range(size)])  56.1 us
    ppermute x12, waiting for transfers between devices, zhop(): lax.ppermute(value, ('zh', 'zl'), [(i, (i + step) % 4) for i in range(4)])  30.5 us
    dot_general x4, matrix products, mm(): return jnp.dot(left, right, preferred_element_type=F32)  25.3 us
    unnamed x147, local copies, waits for them, and re-layouts  21.7 us
    dot_general x4, matrix products, contract_cols(): lax.dot_general(left, right, (((1,), (1,)), ((), ())), preferred_element_...  19.6 us
  transfers between devices with their start and end apart: 71, of which 33 were waited for; matrix products, arithmetic and copies ran while one was open for 17% of the time, Pallas kernels for 0%

profile of v1, /device:TPU:8, one launch (start us, length us, event | category | flops | bytes accessed | tf_op | source)
XLA Modules:
  0.0 688.9 jit_solution(9349200996703684540)
XLA Ops:
  10.0 4.0 collective-permute-start.35
  14.1 8.3 %collective-permute-done.34 = bf16[24,3456]{1,0:T(8,128)(2,1)S(1)} collective-permute-done((bf16[24,3456]{1,0:T(8,128)(2,1)S(1)}, bf16[24,3456]{1,0:T(8,128)(2,1)S(1)}, u32[]{:S(2)}, u32[]{:S(2)}) %collective-permute-start.34) | collective-permute-done | bytes 165920 | tf_op jit(solution)/shard_map/ppermute | solution.py:78
  34.1 12.2 %collective-permute-done.14 = bf16[24,768]{1,0:T(8,128)(2,1)S(1)} collective-permute-done((bf16[24,768]{1,0:T(8,128)(2,1)S(1)}, bf16[24,768]{1,0:T(8,128)(2,1)S(1)}, u32[]{:S(2)}, u32[]{:S(2)}) %collective-permute-start.14) | collective-permute-done | bytes 36896 | tf_op jit(solution)/shard_map/ppermute | solution.py:30
  57.3 4.6 collective-permute-done.15
  75.4 5.2 collective-permute-done.1
  86.1 10.5 %collective-permute-done.24 = bf16[4,2,24,384]{3,2,1,0:T(8,128)(2,1)S(1)} collective-permute-done((bf16[4,2,24,384]{3,2,1,0:T(8,128)(2,1)S(1)}, bf16[4,2,24,384]{3,2,1,0:T(8,128)(2,1)S(1)}, u32[]{:S(2)}, u32[]{:S(2)}) %collective-permute-start.24) | collective-permute-done | bytes 147488 | tf_op jit(solution)/shard_map/ppermute | solution.py:30
  97.1 9.2 %collective-permute-done.25 = bf16[4,2,24,384]{3,2,1,0:T(8,128)(2,1)S(1)} collective-permute-done((bf16[4,2,24,384]{3,2,1,0:T(8,128)(2,1)S(1)}, bf16[4,2,24,384]{3,2,1,0:T(8,128)(2,1)S(1)}, u32[]{:S(2)}, u32[]{:S(2)}) %collective-permute-start.25) | collective-permute-done | bytes 147488 | tf_op jit(solution)/shard_map/ppermute | solution.py:30
  108.4 4.7 collective-permute-done.26
  120.3 4.5 collective-permute-done.19
  129.5 4.3 collective-permute-done.10
  135.3 5.7 collective-permute-done.11
  141.8 4.8 collective-permute-done.12
  146.9 5.4 collective-permute-done.4
  153.5 6.0 collective-permute-done.5
  193.0 8.0 %collective-permute-done.28 = bf16[128,1536]{1,0:T(8,128)(2,1)S(1)} collective-permute-done((bf16[128,1536]{1,0:T(8,128)(2,1)S(1)}, bf16[128,1536]{1,0:T(8,128)(2,1)S(1)}, u32[]{:S(2)}, u32[]{:S(2)}) %collective-permute-start.28) | collective-permute-done | bytes 393248 | tf_op jit(solution)/shard_map/ppermute | solution.py:30
  207.4 8.4 %collective-permute-done.31 = bf16[128,1536]{1,0:T(8,128)(2,1)S(1)} collective-permute-done((bf16[128,1536]{1,0:T(8,128)(2,1)S(1)}, bf16[128,1536]{1,0:T(8,128)(2,1)S(1)}, u32[]{:S(2)}, u32[]{:S(2)}) %collective-permute-start.31) | collective-permute-done | bytes 393248 | tf_op jit(solution)/shard_map/ppermute | solution.py:34
  215.8 6.8 collective-permute-done.30
  230.5 13.5 %fusion.3 = f32[1024,2304]{1,0:T(8,128)} fusion(bf16[1024,1536]{1,0:T(8,128)(2,1)} %constant_dynamic-update-slice_fusion.3, bf16[1536,3456]{1,0:T(8,128)(2,1)} %all-gather.2.cloned.1.call-done), kind=kOutput, calls=%fused_computation.6 | convolution fusion | flops 7247757312 | bytes 19660800 | tf_op jit(solution)/shard_map/dot_general | solution.py:17
  244.0 9.3 %multiply_convert_fusion.1 = (bf16[1024,1152]{1,0:T(8,128)(2,1)S(1)}, bf16[1024,1152]{1,0:T(8,128)(2,1)S(1)}, bf16[1024,1152]{1,0:T(8,128)(2,1)S(1)}) fusion(f32[1024,2304]{1,0:T(8,128)} %fusion.3, bf16[1024,1536]{1,0:T(8,128)(2,1)S(1)} %copy-done.36, bf16[1536,3456]{1,0:T(8,128)(2,1)} %all-gather.2.cloned.1.call-done), kind=kOutput, calls=%fused_computation.13 | convolution fusion | flops 3641573376 | bytes 23199744 | tf_op jit(solution)/shard_map/dot_general | solution.py:17
  253.3 4.6 convolution_convert_fusion.1
  257.9 10.2 %convolution_convert_fusion = bf16[1536,2304]{1,0:T(8,128)(2,1)S(1)} fusion(bf16[1024,1536]{1,0:T(8,128)(2,1)} %constant_dynamic-update-slice_fusion.3, bf16[1024,1152]{1,0:T(8,128)(2,1)S(1)} %get-tuple-element.40, bf16[1024,1152]{1,0:T(8,128)(2,1)S(1)} %get-tuple-element.39), kind=kOutput, calls=%fused_computation.1 | convolution fusion | flops 7260733440 | bytes 14942208 | tf_op jit(solution)/shard_map/dot_general | solution.py:21
  268.1 4.9 pad_maximum_fusion
  273.1 11.4 %fusion.1 = f32[1024,1536]{1,0:T(8,128)S(1)} fusion(bf16[1536,3456]{1,0:T(8,128)(2,1)} %all-gather.2.cloned.1.call-done, bf16[1024,1152]{1,0:T(8,128)(2,1)} %copy-done.65, bf16[1024,1152]{1,0:T(8,128)(2,1)} %copy-done.64), kind=kOutput, calls=%fused_computation.4 | convolution fusion | flops 7257194496 | bytes 18087936 | tf_op jit(solution)/shard_map/dot_general | solution.py:25
  287.9 6.4 fusion.9
  310.2 11.5 %collective-permute-done.46 = bf16[128,1536]{1,0:T(8,128)(2,1)S(1)} collective-permute-done((bf16[128,1536]{1,0:T(8,128)(2,1)S(1)}, bf16[128,1536]{1,0:T(8,128)(2,1)S(1)}, u32[]{:S(2)}, u32[]{:S(2)}) %collective-permute-start.46) | collective-permute-done | bytes 393248 | tf_op jit(solution)/shard_map/ppermute | solution.py:34
  332.6 6.6 collective-permute-done.49
  359.5 8.1 %copy.134 = bf16[1536,1792]{1,0:T(8,128)(2,1)} copy(bf16[1536,1792]{0,1:T(8,128)(2,1)} %pad_maximum_fusion.1) | data formatting | bytes 11010048 | tf_op jit(solution)/shard_map/concatenate | solution.py:247
  379.5 147.3 %psum.22 = f32[1024]{0:T(1024)S(1)} all-reduce(f32[1024]{0:T(1024)S(1)} %convert_reduce_fusion), channel_id=1, replica_groups=mesh['y'=4,'x'=4,'zh'=2,'c'=2,'zl'=2] {'y','x','zh','c'}, use_global_device_ids=true, to_apply=%region_13.14 | all-reduce | flops 1024 | bytes 8192 | tf_op jit(solution)/shard_map/psum | solution.py:252
  528.4 82.3 %all-reduce.1 = (f32[1536]{0:T(1024)}, f32[1536]{0:T(1024)}) all-reduce(f32[1536]{0:T(1024)} %get-tuple-element.14, f32[1536]{0:T(1024)} %get-tuple-element.16), channel_id=1, replica_groups=mesh['y'=4,'x'=4,'zh'=2,'c'=2,'zl'=2] {'y','x','zh','c','zl'}, use_global_device_ids=true, to_apply=%region_11.12 | all-reduce | flops 3072 | bytes 24576 | tf_op jit(solution)/shard_map/psum | solution.py:251
  622.5 13.4 %collective-permute-done.59 = bf16[4,2,24,896]{3,2,1,0:T(8,128)(2,1)S(1)} collective-permute-done((bf16[4,2,24,896]{3,2,1,0:T(8,128)(2,1)S(1)}, bf16[4,2,24,896]{3,2,1,0:T(8,128)(2,1)S(1)}, u32[]{:S(2)}, u32[]{:S(2)}) %collective-permute-start.59) | collective-permute-done | bytes 344096 | tf_op jit(solution)/shard_map/ppermute | solution.py:30
  641.8 6.7 collective-permute-done.54
  670.5 7.9 %collective-permute-done.67 = bf16[24,3456]{1,0:T(8,128)(2,1)S(1)} collective-permute-done((bf16[24,3456]{1,0:T(8,128)(2,1)S(1)}, bf16[24,3456]{1,0:T(8,128)(2,1)S(1)}, u32[]{:S(2)}, u32[]{:S(2)}) %collective-permute-start.67) | collective-permute-done | bytes 165920 | tf_op jit(solution)/shard_map/ppermute | solution.py:78
  (421 shorter events, 216.3 us)
Async XLA Ops:
  7.2 223.3 %all-gather.2.cloned.1.call-start = ((), (), s32[]{:S(2)}) async-start(), calls=%async_computation.1 | async-start | bytes 11280384 | tf_op jit(solution)/shard_map/all_gather | solution.py:159
  23.3 641.5 %reduce-scatter.2.cloned.1.call-start = ((), (), s32[]{:S(2)}) async-start(), calls=%async_computation.2 | async-start | bytes 11280384 | tf_op jit(solution)/shard_map/reduce_scatter | solution.py:210
  24.2 167.3 %collective-permute-start.43 = (bf16[128,1536]{1,0:T(8,128)(2,1)S(1)}, bf16[128,1536]{1,0:T(8,128)(2,1)}, u32[]{:S(2)}, u32[]{:S(2)}) collective-permute-start(bf16[128,1536]{1,0:T(8,128)(2,1)S(1)} %get-tuple-element.24), channel_id=1, source_target_pairs={{0,4},{1,5},{4,0},{5,1},{2,6},{3,7},{6,2},{7,3},{8,12},{9,13},{12,... | collective-permute-start | bytes 1179656 | tf_op jit(solution)/shard_map/ppermute | solution.py:34
  27.4 164.1 %collective-permute-start.42 = (bf16[128,1536]{1,0:T(8,128)(2,1)S(1)}, bf16[128,1536]{1,0:T(8,128)(2,1)}, u32[]{:S(2)}, u32[]{:S(2)}) collective-permute-start(bf16[128,1536]{1,0:T(8,128)(2,1)S(1)} %get-tuple-element.24), channel_id=1, source_target_pairs={{0,5},{1,0},{4,1},{5,4},{2,7},{3,2},{6,3},{7,6},{8,13},{9,8},{12,9... | collective-permute-start | bytes 1179656 | tf_op jit(solution)/shard_map/ppermute | solution.py:34
  28.1 163.4 %collective-permute-start.41 = (bf16[128,1536]{1,0:T(8,128)(2,1)S(1)}, bf16[128,1536]{1,0:T(8,128)(2,1)}, u32[]{:S(2)}, u32[]{:S(2)}) collective-permute-start(bf16[128,1536]{1,0:T(8,128)(2,1)S(1)} %get-tuple-element.24), channel_id=1, source_target_pairs={{0,1},{1,4},{4,5},{5,0},{2,3},{3,6},{6,7},{7,2},{8,9},{9,12},{12,1... | collective-permute-start | bytes 1179656 | tf_op jit(solution)/shard_map/ppermute | solution.py:34
  29.5 16.8 %collective-permute-start.14 = (bf16[24,768]{1,0:T(8,128)(2,1)S(1)}, bf16[24,768]{1,0:T(8,128)(2,1)S(1)}, u32[]{:S(2)}, u32[]{:S(2)}) collective-permute-start(bf16[24,768]{1,0:T(8,128)(2,1)S(1)} %bitcast.325), channel_id=1, source_target_pairs={{0,4},{4,0},{1,5},{5,1},{2,6},{6,2},{3,7},{7,3},{8,12},{12,8},{9,1... | collective-permute-start | bytes 110600 | tf_op jit(solution)/shard_map/ppermute | solution.py:30
  30.6 17.5 %collective-permute-start = (bf16[24,1024]{1,0:T(8,128)(2,1)S(1)}, bf16[24,1024]{1,0:T(8,128)(2,1)S(1)}, u32[]{:S(2)}, u32[]{:S(2)}) collective-permute-start(bf16[24,1024]{1,0:T(8,128)(2,1)S(1)} %constant_dynamic-update-slice_fusion), channel_id=1, source_target_pairs={{0,4},{4,0},{1,5},{5,1},{2,6},{6,2},{3,7},{7,3},{8,12},{12,8},{9,1... | collective-permute-start | bytes 147464 | tf_op jit(solution)/shard_map/ppermute | solution.py:30
  82.0 44.6 %collective-permute-start.20 = (bf16[4,2,24,384]{3,2,1,0:T(8,128)(2,1)S(1)}, bf16[4,2,24,384]{3,2,1,0:T(8,128)(2,1)S(1)}, u32[]{:S(2)}, u32[]{:S(2)}) collective-permute-start(bf16[4,2,24,384]{3,2,1,0:T(8,128)(2,1)S(1)} %bitcast_dynamic-update-slice_fusion.34), channel_id=1, source_target_pairs={{0,96},{32,0},{64,32},{96,64},{1,97},{33,1},{65,33},{97,65},{2,98}... | collective-permute-start | bytes 442376 | tf_op jit(solution)/shard_map/ppermute | solution.py:30
  124.8 34.7 %collective-permute-start.6 = (bf16[4,2,24,512]{3,2,1,0:T(8,128)(2,1)S(1)}, bf16[4,2,24,512]{3,2,1,0:T(8,128)(2,1)S(1)}, u32[]{:S(2)}, u32[]{:S(2)}) collective-permute-start(bf16[4,2,24,512]{3,2,1,0:T(8,128)(2,1)S(1)} %bitcast_dynamic-update-slice_fusion.26), channel_id=1, source_target_pairs={{0,96},{32,0},{64,32},{96,64},{1,97},{33,1},{65,33},{97,65},{2,98}... | collective-permute-start | bytes 589832 | tf_op jit(solution)/shard_map/ppermute | solution.py:30
  192.9 33.4 %collective-permute-start.44 = (bf16[512,1536]{1,0:T(8,128)(2,1)S(1)}, bf16[512,1536]{1,0:T(8,128)(2,1)S(1)}, u32[]{:S(2)}, u32[]{:S(2)}) collective-permute-start(bf16[512,1536]{1,0:T(8,128)(2,1)S(1)} %pad_maximum_fusion.9), channel_id=1, source_target_pairs={{0,2},{2,0},{1,3},{3,1},{4,6},{6,4},{5,7},{7,5},{8,10},{10,8},{9,1... | collective-permute-start | bytes 4718600 | tf_op jit(solution)/shard_map/ppermute | solution.py:30
  202.2 13.6 %collective-permute-start.31 = (bf16[128,1536]{1,0:T(8,128)(2,1)S(1)}, bf16[128,1536]{1,0:T(8,128)(2,1)S(1)}, u32[]{:S(2)}, u32[]{:S(2)}) collective-permute-start(bf16[128,1536]{1,0:T(8,128)(2,1)S(1)} %get-tuple-element.28), channel_id=1, source_target_pairs={{0,4},{1,5},{4,0},{5,1},{2,6},{3,7},{6,2},{7,3},{8,12},{9,13},{12,... | collective-permute-start | bytes 1179656 | tf_op jit(solution)/shard_map/ppermute | solution.py:34
  205.4 17.3 %collective-permute-start.30 = (bf16[128,1536]{1,0:T(8,128)(2,1)S(1)}, bf16[128,1536]{1,0:T(8,128)(2,1)S(1)}, u32[]{:S(2)}, u32[]{:S(2)}) collective-permute-start(bf16[128,1536]{1,0:T(8,128)(2,1)S(1)} %get-tuple-element.28), channel_id=1, source_target_pairs={{0,5},{1,0},{4,1},{5,4},{2,7},{3,2},{6,3},{7,6},{8,13},{9,8},{12,9... | collective-permute-start | bytes 1179656 | tf_op jit(solution)/shard_map/ppermute | solution.py:34
  206.4 16.2 %collective-permute-start.29 = (bf16[128,1536]{1,0:T(8,128)(2,1)S(1)}, bf16[128,1536]{1,0:T(8,128)(2,1)S(1)}, u32[]{:S(2)}, u32[]{:S(2)}) collective-permute-start(bf16[128,1536]{1,0:T(8,128)(2,1)S(1)} %get-tuple-element.28), channel_id=1, source_target_pairs={{0,1},{1,4},{4,5},{5,0},{2,3},{3,6},{6,7},{7,2},{8,9},{9,12},{12,1... | collective-permute-start | bytes 1179656 | tf_op jit(solution)/shard_map/ppermute | solution.py:34
  285.9 12.9 %collective-permute-start.45 = (bf16[512,1536]{1,0:T(8,128)(2,1)}, bf16[512,1536]{1,0:T(8,128)(2,1)}, u32[]{:S(2)}, u32[]{:S(2)}) collective-permute-start(bf16[512,1536]{1,0:T(8,128)(2,1)} %slice.258), channel_id=1, source_target_pairs={{0,2},{2,0},{1,3},{3,1},{4,6},{6,4},{5,7},{7,5},{8,10},{10,8},{9,1... | collective-permute-start | bytes 4718600 | tf_op jit(solution)/shard_map/ppermute | solution.py:30
  302.0 19.7 %collective-permute-start.46 = (bf16[128,1536]{1,0:T(8,128)(2,1)S(1)}, bf16[128,1536]{1,0:T(8,128)(2,1)S(1)}, u32[]{:S(2)}, u32[]{:S(2)}) collective-permute-start(bf16[128,1536]{1,0:T(8,128)(2,1)S(1)} %get-tuple-element.50), channel_id=1, source_target_pairs={{0,5},{1,0},{4,1},{5,4},{2,7},{3,2},{6,3},{7,6},{8,13},{9,8},{12,9... | collective-permute-start | bytes 1179656 | tf_op jit(solution)/shard_map/ppermute | solution.py:34
  304.9 16.9 %collective-permute-start.48 = (bf16[128,1536]{1,0:T(8,128)(2,1)S(1)}, bf16[128,1536]{1,0:T(8,128)(2,1)S(1)}, u32[]{:S(2)}, u32[]{:S(2)}) collective-permute-start(bf16[128,1536]{1,0:T(8,128)(2,1)S(1)} %get-tuple-element.51), channel_id=1, source_target_pairs={{0,4},{1,5},{4,0},{5,1},{2,6},{3,7},{6,2},{7,3},{8,12},{9,13},{12,... | collective-permute-start | bytes 1179656 | tf_op jit(solution)/shard_map/ppermute | solution.py:34
  305.6 19.8 %collective-permute-start.47 = (bf16[128,1536]{1,0:T(8,128)(2,1)S(1)}, bf16[128,1536]{1,0:T(8,128)(2,1)S(1)}, u32[]{:S(2)}, u32[]{:S(2)}) collective-permute-start(bf16[128,1536]{1,0:T(8,128)(2,1)S(1)} %get-tuple-element.52), channel_id=1, source_target_pairs={{0,1},{1,4},{4,5},{5,0},{2,3},{3,6},{6,7},{7,2},{8,9},{9,12},{12,1... | collective-permute-start | bytes 1179656 | tf_op jit(solution)/shard_map/ppermute | solution.py:34
  328.3 45.1 %collective-permute-start.37 = (bf16[128,1536]{1,0:T(8,128)(2,1)}, bf16[128,1536]{1,0:T(8,128)(2,1)}, u32[]{:S(2)}, u32[]{:S(2)}) collective-permute-start(bf16[128,1536]{1,0:T(8,128)(2,1)} %get-tuple-element.53), channel_id=1, source_target_pairs={{0,5},{1,0},{4,1},{5,4},{2,7},{3,2},{6,3},{7,6},{8,13},{9,8},{12,9... | collective-permute-start | bytes 1179656 | tf_op jit(solution)/shard_map/ppermute | solution.py:34
  329.7 43.7 %collective-permute-start.39 = (bf16[128,1536]{1,0:T(8,128)(2,1)}, bf16[128,1536]{1,0:T(8,128)(2,1)}, u32[]{:S(2)}, u32[]{:S(2)}) collective-permute-start(bf16[128,1536]{1,0:T(8,128)(2,1)} %get-tuple-element.54), channel_id=1, source_target_pairs={{0,4},{1,5},{4,0},{5,1},{2,6},{3,7},{6,2},{7,3},{8,12},{9,13},{12,... | collective-permute-start | bytes 1179656 | tf_op jit(solution)/shard_map/ppermute | solution.py:34
  332.4 41.0 %collective-permute-start.38 = (bf16[128,1536]{1,0:T(8,128)(2,1)}, bf16[128,1536]{1,0:T(8,128)(2,1)}, u32[]{:S(2)}, u32[]{:S(2)}) collective-permute-start(bf16[128,1536]{1,0:T(8,128)(2,1)} %get-tuple-element.55), channel_id=1, source_target_pairs={{0,1},{1,4},{4,5},{5,0},{2,3},{3,6},{6,7},{7,2},{8,9},{9,12},{12,1... | collective-permute-start | bytes 1179656 | tf_op jit(solution)/shard_map/ppermute | solution.py:34
  354.7 16.8 %collective-permute-start.50 = (bf16[128,1536]{1,0:T(8,128)(2,1)}, bf16[128,1536]{1,0:T(8,128)(2,1)}, u32[]{:S(2)}, u32[]{:S(2)}) collective-permute-start(bf16[128,1536]{1,0:T(8,128)(2,1)} %dynamic-slice_convert_fusion), channel_id=1, source_target_pairs={{0,1},{1,0},{2,3},{3,2},{4,5},{5,4},{6,7},{7,6},{8,9},{9,8},{10,11... | collective-permute-start | bytes 1179656 | tf_op jit(solution)/shard_map/ppermute | solution.py:30
  371.2 242.0 %collective-permute-start.52 = (bf16[4,4,2,24,1792]{4,3,2,1,0:T(8,128)(2,1)}, bf16[4,4,2,24,1792]{4,3,2,1,0:T(8,128)(2,1)}, u32[]{:S(2)}, u32[]{:S(2)}) collective-permute-start(bf16[4,4,2,24,1792]{4,3,2,1,0:T(8,128)(2,1)} %dynamic-slice_bitcast_fusion), channel_id=1, source_target_pairs={{0,2},{2,0},{1,3},{3,1},{4,6},{6,4},{5,7},{7,5},{8,10},{10,8},{9,1... | collective-permute-start | bytes 8257544 | tf_op jit(solution)/shard_map/ppermute | solution.py:30
  376.5 234.2 %collective-permute-start.51 = (bf16[128,1536]{1,0:T(8,128)(2,1)}, bf16[128,1536]{1,0:T(8,128)(2,1)S(1)}, u32[]{:S(2)}, u32[]{:S(2)}) collective-permute-start(bf16[128,1536]{1,0:T(8,128)(2,1)} %get-tuple-element.69), channel_id=1, source_target_pairs={{0,1},{1,0},{2,3},{3,2},{4,5},{5,4},{6,7},{7,6},{8,9},{9,8},{10,11... | collective-permute-start | bytes 1179656 | tf_op jit(solution)/shard_map/ppermute | solution.py:30
  527.3 92.9 %collective-permute-start.40 = (bf16[128,1536]{1,0:T(8,128)(2,1)S(1)}, bf16[128,1536]{1,0:T(8,128)(2,1)S(1)}, u32[]{:S(2)}, u32[]{:S(2)}) collective-permute-start(bf16[128,1536]{1,0:T(8,128)(2,1)S(1)} %get-tuple-element.70), channel_id=1, source_target_pairs={{0,1},{1,0},{2,3},{3,2},{4,5},{5,4},{6,7},{7,6},{8,9},{9,8},{10,11... | collective-permute-start | bytes 1179656 | tf_op jit(solution)/shard_map/ppermute | solution.py:30
  616.9 19.0 %collective-permute-start.59 = (bf16[4,2,24,896]{3,2,1,0:T(8,128)(2,1)S(1)}, bf16[4,2,24,896]{3,2,1,0:T(8,128)(2,1)S(1)}, u32[]{:S(2)}, u32[]{:S(2)}) collective-permute-start(bf16[4,2,24,896]{3,2,1,0:T(8,128)(2,1)S(1)} %get-tuple-element.56), channel_id=1, source_target_pairs={{0,8},{8,16},{16,24},{24,0},{1,9},{9,17},{17,25},{25,1},{2,10},{10... | collective-permute-start | bytes 1032200 | tf_op jit(solution)/shard_map/ppermute | solution.py:30
  617.0 19.1 %collective-permute-start.61 = (bf16[4,2,24,896]{3,2,1,0:T(8,128)(2,1)S(1)}, bf16[4,2,24,896]{3,2,1,0:T(8,128)(2,1)S(1)}, u32[]{:S(2)}, u32[]{:S(2)}) collective-permute-start(bf16[4,2,24,896]{3,2,1,0:T(8,128)(2,1)S(1)} %get-tuple-element.57), channel_id=1, source_target_pairs={{0,24},{8,0},{16,8},{24,16},{1,25},{9,1},{17,9},{25,17},{2,26},{10... | collective-permute-start | bytes 1032200 | tf_op jit(solution)/shard_map/ppermute | solution.py:30
  620.2 15.9 %collective-permute-start.60 = (bf16[4,2,24,896]{3,2,1,0:T(8,128)(2,1)S(1)}, bf16[4,2,24,896]{3,2,1,0:T(8,128)(2,1)S(1)}, u32[]{:S(2)}, u32[]{:S(2)}) collective-permute-start(bf16[4,2,24,896]{3,2,1,0:T(8,128)(2,1)S(1)} %get-tuple-element.58), channel_id=1, source_target_pairs={{0,16},{8,24},{16,0},{24,8},{1,17},{9,25},{17,1},{25,9},{2,18},{10... | collective-permute-start | bytes 1032200 | tf_op jit(solution)/shard_map/ppermute | solution.py:30
  620.4 18.0 %collective-permute-start.53 = (bf16[4,2,24,896]{3,2,1,0:T(8,128)(2,1)S(1)}, bf16[4,2,24,896]{3,2,1,0:T(8,128)(2,1)S(1)}, u32[]{:S(2)}, u32[]{:S(2)}) collective-permute-start(bf16[4,2,24,896]{3,2,1,0:T(8,128)(2,1)S(1)} %get-tuple-element.59), channel_id=1, source_target_pairs={{0,32},{32,64},{64,96},{96,0},{1,33},{33,65},{65,97},{97,1},{2,34}... | collective-permute-start | bytes 1032200 | tf_op jit(solution)/shard_map/ppermute | solution.py:30
  621.3 20.5 %collective-permute-start.55 = (bf16[4,2,24,896]{3,2,1,0:T(8,128)(2,1)S(1)}, bf16[4,2,24,896]{3,2,1,0:T(8,128)(2,1)S(1)}, u32[]{:S(2)}, u32[]{:S(2)}) collective-permute-start(bf16[4,2,24,896]{3,2,1,0:T(8,128)(2,1)S(1)} %get-tuple-element.60), channel_id=1, source_target_pairs={{0,96},{32,0},{64,32},{96,64},{1,97},{33,1},{65,33},{97,65},{2,98}... | collective-permute-start | bytes 1032200 | tf_op jit(solution)/shard_map/ppermute | solution.py:30
  636.3 15.7 %collective-permute-start.62 = (bf16[2,24,896]{2,1,0:T(8,128)(2,1)S(1)}, bf16[2,24,896]{2,1,0:T(8,128)(2,1)S(1)}, u32[]{:S(2)}, u32[]{:S(2)}) collective-permute-start(bf16[2,24,896]{2,1,0:T(8,128)(2,1)S(1)} %get-tuple-element.85), channel_id=1, source_target_pairs={{0,32},{32,64},{64,96},{96,0},{1,33},{33,65},{65,97},{97,1},{2,34}... | collective-permute-start | bytes 258056 | tf_op jit(solution)/shard_map/ppermute | solution.py:30
  636.5 15.5 %collective-permute-start.64 = (bf16[2,24,896]{2,1,0:T(8,128)(2,1)S(1)}, bf16[2,24,896]{2,1,0:T(8,128)(2,1)S(1)}, u32[]{:S(2)}, u32[]{:S(2)}) collective-permute-start(bf16[2,24,896]{2,1,0:T(8,128)(2,1)S(1)} %get-tuple-element.86), channel_id=1, source_target_pairs={{0,96},{32,0},{64,32},{96,64},{1,97},{33,1},{65,33},{97,65},{2,98}... | collective-permute-start | bytes 258056 | tf_op jit(solution)/shard_map/ppermute | solution.py:30
  638.4 13.6 %collective-permute-start.63 = (bf16[2,24,896]{2,1,0:T(8,128)(2,1)S(1)}, bf16[2,24,896]{2,1,0:T(8,128)(2,1)S(1)}, u32[]{:S(2)}, u32[]{:S(2)}) collective-permute-start(bf16[2,24,896]{2,1,0:T(8,128)(2,1)S(1)} %get-tuple-element.87), channel_id=1, source_target_pairs={{0,64},{32,96},{64,0},{96,32},{1,65},{33,97},{65,1},{97,33},{2,66}... | collective-permute-start | bytes 258056 | tf_op jit(solution)/shard_map/ppermute | solution.py:30
  (107 other events, 842.2 us)
Sparse Core Ops, SparseCore 0:
  23.5 90.8 all-gather.1
  273.2 89.6 reduce-scatter.1

commit v2 on v1

v2 whole, which is shorter than its diff:
```python
import jax
import jax.numpy as jnp
from jax import lax
from jax.experimental import pallas as pl
from jax.experimental.pallas import tpu as pltpu
from jax.sharding import Mesh, PartitionSpec as P

HD = 128
BF = jnp.bfloat16
F32 = jnp.float32
rope_base = 10000.0
norm_eps = 1e-06
WIDE = ("y", "x", "zh", "c")
EVERY = ("y", "x", "zh", "c", "zl")
SLICE = 1152
ATT = 896
LEFT = 512
HEADS = 6


def mm(left, right):
    return jnp.dot(left, right, preferred_element_type=F32)


def contract_rows(left, right):
    return lax.dot_general(left, right, (((0,), (0,)), ((), ())), preferred_element_type=F32)


def contract_cols(left, right):
    return lax.dot_general(left, right, (((1,), (1,)), ((), ())), preferred_element_type=F32)


def hop(value, axis, step):
    size = lax.axis_size(axis)
    return lax.ppermute(value, axis, [(i, (i + step) % size) for i in range(size)])


def zhop(value, step):
    return lax.ppermute(value, ("zh", "zl"), [(i, (i + step) % 4) for i in range(4)])


def put(whole, piece, spots):
    return lax.dynamic_update_slice(whole, piece, spots)


def ring_pieces(value, axis):
    return [(0, value)] + [(k, hop(value, axis, k)) for k in (1, 3, 2)]


def pair(mine, theirs, side, dim):
    first = jnp.where(side == 0, mine, theirs)
    second = jnp.where(side == 0, theirs, mine)
    return jnp.stack([first, second], dim)


def quad_hop(value, flip):
    return lax.ppermute(value, ("zh", "c"), [(i, i ^ flip) for i in range(4)])


def gather_attn(value, spot):
    y, x, zh, c = spot
    me = zh * 2 + c
    mine = lax.dynamic_index_in_dim(value, c, 0)
    other = lax.dynamic_index_in_dim(value, 1 - c, 0)
    block = jnp.zeros((4, 24, ATT), value.dtype)
    block = put(block, mine, (me, 0, 0))
    for flip, sent in ((1, other), (2, mine), (3, other)):
        block = put(block, quad_hop(sent, flip), (me ^ flip, 0, 0))
    block = block.reshape(1, 96, ATT)
    left = jnp.zeros((4, 96, LEFT), value.dtype)
    for k, piece in ring_pieces(block[..., :LEFT], "x"):
        left = put(left, piece, ((x - k) % 4, 0, 0))
    right = jnp.zeros((4, 96, ATT - LEFT), value.dtype)
    for k, piece in ring_pieces(block[..., LEFT:], "y"):
        right = put(right, piece, ((y - k) % 4, 0, 0))
    half = jnp.zeros((4, 4, 96, ATT), value.dtype)
    for k, piece in ring_pieces(left[None], "y"):
        half = put(half, piece, ((y - k) % 4, 0, 0, 0))
    for k, piece in ring_pieces(right[:, None], "x"):
        half = put(half, piece, (0, (x - k) % 4, 0, LEFT))
    half = half.reshape(1, 1536, ATT)
    whole = jnp.zeros((2, 1536, ATT), value.dtype)
    whole = put(whole, half, (c, 0, 0))
    return put(whole, hop(half, "c", 1), (1 - c, 0, 0))


def ring_sum(value, axis, me, dim):
    def block(k):
        return lax.dynamic_index_in_dim(value, (me + k) % 4, dim, keepdims=False)

    total = block(0).astype(F32)
    for k in (1, 3, 2):
        total = total + hop(block(k), axis, k).astype(F32)
    return total


def scatter_attn(value, spot):
    y, x, zh, c = spot
    me = zh * 2 + c
    mine = lax.dynamic_index_in_dim(value, c, 0, keepdims=False)
    other = lax.dynamic_index_in_dim(value, 1 - c, 0, keepdims=False)
    part = (mine.astype(F32) + hop(other, "c", 1).astype(F32)).astype(BF)
    part = part.reshape(4, 4, 96, ATT)
    left = ring_sum(part[..., :LEFT], "y", y, 0).astype(BF)
    right = ring_sum(part[..., LEFT:], "x", x, 1).astype(BF)
    left = ring_sum(left, "x", x, 0)
    right = ring_sum(right, "y", y, 0)
    part = jnp.concatenate([left, right], -1).reshape(4, 24, ATT)

    def block(flip):
        return lax.dynamic_index_in_dim(part, me ^ flip, 0, keepdims=False)

    got = [quad_hop(block(flip).astype(BF), flip).astype(F32) for flip in (1, 2, 3)]
    return pair(block(0) + got[1], got[0] + got[2], c, 0)


def sum_vectors(value, spot):
    y, x, zh, c = spot
    zl = lax.axis_index("zl")
    value = value + hop(value, "c", 1)
    for axis, me in (("x", x), ("y", y)):
        whole = jnp.zeros((4,) + value.shape, F32)
        for k, piece in ring_pieces(value, axis):
            whole = put(whole, piece[None], ((me - k) % 4, 0, 0))
        value = (whole[0] + whole[1]) + (whole[2] + whole[3])
    value = value + hop(value, "zh", 1)
    return jnp.concatenate([value[:24] + hop(value[:24], "zl", 1), value[24:]], 0)


def trade(blocks, zh, c):
    me = zh * 2 + c
    got = []
    for k in range(4):
        block = lax.dynamic_index_in_dim(blocks, me ^ k, 0, keepdims=False)
        if k:
            block = lax.ppermute(block, ("zh", "c"), [(i, i ^ k) for i in range(4)])
        got.append(block)
    whole = jnp.zeros(blocks.shape, blocks.dtype)
    for k in range(4):
        whole = lax.dynamic_update_index_in_dim(whole, got[k], me ^ k, 0)
    return whole


def gather_tokens(value):
    ring = jnp.concatenate([value, zhop(value, 1), zhop(value, 3), zhop(value, 2)], 0)
    return jnp.concatenate([ring, hop(ring, "c", 1)], 0)


def sum_tokens(part):
    half = part.shape[0] // 2
    quarter = half // 4
    mine = part[:half].astype(F32) + hop(part[half:].astype(BF), "c", 1).astype(F32)
    sent = mine.astype(BF)
    back = zhop(sent[quarter : 2 * quarter], 3)
    ahead = zhop(sent[2 * quarter : 3 * quarter], 1)
    far = zhop(sent[3 * quarter :], 2)
    return mine[:quarter] + back.astype(F32) + ahead.astype(F32) + far.astype(F32)


def halves(side, value, mine_ref, theirs_ref):
    half = value.shape[0] // 2
    low, high = value[:half], value[half:]
    first = side == 0
    mine_ref[...] = jnp.where(first, low, high)
    theirs_ref[...] = jnp.where(first, high, low).astype(BF)


def turn(value, cosine, sine):
    return value * cosine + pltpu.roll(value, HD // 2, 1) * sine


def attention_kernel(
    side, h, w, bias, cosine, sine, keep, mine, theirs, attended, qkv_out, probs_out
):
    scale = HD ** (-0.5)
    cos, sin = cosine[...], sine[...]
    allowed = keep[...] > 0.5
    q_cols = HEADS * HD
    first = mm(h[...], w[0]) + bias[:, :ATT]
    keys = turn(first[:, q_cols:], cos, sin).astype(BF)
    values = (mm(h[...], w[1, :, :HD]) + bias[:, ATT:]).astype(BF)
    qkv_out[:, q_cols : q_cols + HD] = keys
    qkv_out[:, q_cols + HD :] = values
    for g in range(HEADS):
        cols = slice(g * HD, (g + 1) * HD)
        query = turn(first[:, cols], cos, sin).astype(BF)
        qkv_out[:, cols] = query
        logits = jnp.where(allowed, contract_cols(query, keys) * scale, -1000000000.0)
        expo = jnp.exp(logits - jnp.max(logits, axis=-1, keepdims=True))
        probs = expo / jnp.sum(expo, axis=-1, keepdims=True)
        probs_out[g] = probs
        attended[:, cols] = mm(probs.astype(BF), values).astype(BF)
    halves(side[0], contract_cols(attended[...], w[1, :, HD:]), mine, theirs)


def attention_forward(side, h, w, bias, cosine, sine, keep):
    rows, d = h.shape
    return pl.pallas_call(
        attention_kernel,
        in_specs=[pl.BlockSpec(memory_space=pltpu.SMEM)]
        + [pl.BlockSpec(memory_space=pltpu.VMEM)] * 6,
        out_shape=(
            jax.ShapeDtypeStruct((rows // 2, d), F32),
            jax.ShapeDtypeStruct((rows // 2, d), BF),
            jax.ShapeDtypeStruct((rows, HEADS * HD), BF),
            jax.ShapeDtypeStruct((rows, (HEADS + 2) * HD), BF),
            jax.ShapeDtypeStruct((HEADS, rows, rows), F32),
        ),
        compiler_params=pltpu.CompilerParams(vmem_limit_bytes=48 * 2**20),
        cost_estimate=pl.CostEstimate(
            flops=2_200_000_000, bytes_accessed=12_000_000, transcendentals=400_000
        ),
    )(side, h, w, bias, cosine, sine, keep)


def attention_back_kernel(
    side, branch, h, w, attended, qkv, probs, cosine, sine, mine, theirs, grads, bias, grad_qkv
):
    scale = HD ** (-0.5)
    cos, sin = cosine[...], -sine[...]
    q_cols = HEADS * HD
    keys = qkv[:, q_cols : q_cols + HD]
    values = qkv[:, q_cols + HD :]
    grad_att = mm(branch[...], w[1, :, HD:]).astype(BF)
    grad_key = jnp.zeros((branch.shape[0], HD), F32)
    grad_value = jnp.zeros((branch.shape[0], HD), F32)
    for g in range(HEADS):
        cols = slice(g * HD, (g + 1) * HD)
        grad_head = grad_att[:, cols]
        grad_probs = contract_cols(grad_head, values)
        prob = probs[g]
        inner = jnp.sum(prob * grad_probs, axis=-1, keepdims=True)
        grad_logits = (prob * (grad_probs - inner)).astype(BF)
        grad_query = mm(grad_logits, keys) * scale
        grad_qkv[:, cols] = turn(grad_query, cos, sin).astype(BF)
        grad_key += contract_rows(grad_logits, qkv[:, cols])
        grad_value += contract_rows(prob.astype(BF), grad_head)
    grad_qkv[:, q_cols : q_cols + HD] = turn(grad_key * scale, cos, sin).astype(BF)
    grad_qkv[:, q_cols + HD :] = grad_value.astype(BF)
    bias[...] = jnp.sum(grad_qkv[...].astype(F32), axis=0, keepdims=True)
    grads[0] = contract_rows(h[...], grad_qkv[:, :ATT]).astype(BF)
    grads[1, :, :HD] = contract_rows(h[...], grad_qkv[:, ATT:]).astype(BF)
    grads[1, :, HD:] = contract_rows(branch[...], attended[...]).astype(BF)
    grad_h = contract_cols(grad_qkv[:, :ATT], w[0])
    grad_h += contract_cols(grad_qkv[:, ATT:], w[1, :, :HD])
    halves(side[0], grad_h, mine, theirs)


def attention_backward(side, branch, h, w, attended, qkv, probs, cosine, sine):
    rows, d = h.shape
    return pl.pallas_call(
        attention_back_kernel,
        in_specs=[pl.BlockSpec(memory_space=pltpu.SMEM)]
        + [pl.BlockSpec(memory_space=pltpu.VMEM)] * 8,
        out_shape=(
            jax.ShapeDtypeStruct((rows // 2, d), F32),
            jax.ShapeDtypeStruct((rows // 2, d), BF),
            jax.ShapeDtypeStruct(w.shape, BF),
            jax.ShapeDtypeStruct((1, (HEADS + 2) * HD), F32),
        ),
        scratch_shapes=[pltpu.VMEM((rows, (HEADS + 2) * HD), BF)],
        compiler_params=pltpu.CompilerParams(vmem_limit_bytes=48 * 2**20),
        cost_estimate=pl.CostEstimate(
            flops=4_300_000_000, bytes_accessed=20_000_000, transcendentals=0
        ),
    )(side, branch, h, w, attended, qkv, probs, cosine, sine)


def doc_layout(lengths, count):
    ends = jnp.cumsum(lengths)
    starts = ends - lengths
    place = jnp.arange(count, dtype=jnp.int32)
    segment = jnp.sum((place[:, None] >= ends[None, :]).astype(jnp.int32), axis=1)
    labels = jnp.arange(lengths.shape[0], dtype=jnp.int32)
    first = jnp.sum(jnp.where(segment[:, None] == labels[None, :], starts[None, :], 0), axis=1)
    return (segment, place - first, place)


def own_rows(value, side):
    half = value.shape[0] // 2
    return lax.dynamic_slice_in_dim(value, side * half, half, 0)


def both_rows(mine, zl):
    return pair(mine, hop(mine, "zl", 1), zl, 0).reshape(2 * mine.shape[0], mine.shape[1])


def on_device(
    tokens,
    doc_lengths,
    norm_gain1,
    w_query,
    b_query,
    w_key,
    b_key,
    w_value,
    b_value,
    w_out,
    norm_gain2,
    w_gate,
    w_up,
    w_down,
    out_grad,
):
    y, x, zh, c, zl = (lax.axis_index(axis) for axis in EVERY)
    spot = (y, x, zh, c)
    rows = tokens.shape[0]
    hidden_units = w_gate.shape[1]
    pad = 4 * SLICE - hidden_units

    side = zl.reshape(1)
    attn = jnp.concatenate([w_query, w_key, w_value, w_out.T], 1)
    attn = jnp.stack([attn[:, :ATT], attn[:, ATT:]], 0)
    attn_full = gather_attn(attn, spot)
    ffn = jnp.stack([w_gate, w_up, w_down.T], 1)
    ffn = jnp.pad(ffn, ((0, 0), (0, 0), (0, pad))).reshape(24, 3, 4, SLICE)
    ffn = trade(ffn.transpose(2, 0, 1, 3).reshape(4, 24, 3 * SLICE), zh, c)
    ffn_full = lax.all_gather(ffn.reshape(96, 3 * SLICE), ("y", "x"), axis=0, tiled=True)
    gate_up_full, down_full = ffn_full[:, : 2 * SLICE], ffn_full[:, 2 * SLICE :]
    grad_all = gather_tokens(own_rows(out_grad, zl))

    segment, position, place = doc_layout(doc_lengths[0], rows)
    inverse = rope_base ** (-jnp.arange(0, HD, 2, dtype=F32) / HD)
    angle = position.astype(F32)[:, None] * inverse[None, :]
    cosine, sine = jnp.cos(angle), jnp.sin(angle)
    cosine = jnp.concatenate([cosine, cosine], 1)
    sine = jnp.concatenate([-sine, sine], 1)
    keep = (segment[:, None] == segment[None, :]) & (place[None, :] <= place[:, None])
    inputs = tokens.astype(F32)
    factor_one = lax.rsqrt(jnp.mean(inputs * inputs, axis=-1, keepdims=True) + norm_eps)
    normed_one = inputs * factor_one
    h_one = (normed_one * norm_gain1).astype(BF)
    bias = jnp.concatenate([b_query, b_key, b_value])[None]
    mine, theirs, attended, qkv, probs = attention_forward(
        side, h_one, attn_full, bias, cosine, sine, keep.astype(F32)
    )
    theirs = hop(theirs, "zl", 1)
    resid = own_rows(tokens, zl).astype(F32) + mine + theirs.astype(F32)

    factor_two = lax.rsqrt(jnp.mean(resid * resid, axis=-1, keepdims=True) + norm_eps)
    normed_two = resid * factor_two
    h_two = gather_tokens((normed_two * norm_gain2).astype(BF))
    gate_up = mm(h_two, gate_up_full)
    grad_hidden = mm(grad_all, down_full)
    gate, up_act = gate_up[:, :SLICE], gate_up[:, SLICE:]
    sigma = jax.nn.sigmoid(gate)
    swish = gate * sigma
    hidden = (swish * up_act).astype(BF)
    grad_gate_act = (grad_hidden * up_act * sigma * (1.0 + gate * (1.0 - sigma))).astype(BF)
    grad_up_act = (grad_hidden * swish).astype(BF)
    grad_act = jnp.concatenate([grad_gate_act, grad_up_act], 1)
    grad_h_two = sum_tokens(contract_cols(grad_act, gate_up_full))
    d_ffn = jnp.concatenate(
        [contract_rows(h_two, grad_act).astype(BF), contract_rows(grad_all, hidden).astype(BF)], 1
    )
    mixed = (resid + sum_tokens(contract_cols(hidden, down_full))).astype(BF)
    mixed_out = both_rows(mixed, zl)
    d_ffn = lax.psum_scatter(d_ffn, ("y", "x"), scatter_dimension=0, tiled=True)
    d_ffn = trade(d_ffn.reshape(4, 24, 3 * SLICE), zh, c).astype(F32)
    d_ffn = d_ffn.reshape(4, 24, 3, SLICE).transpose(2, 1, 0, 3).reshape(3, 24, 4 * SLICE)
    d_gate, d_up, d_down = (d_ffn[i, :, :hidden_units] for i in range(3))

    gain_two_term = jnp.sum(grad_h_two * normed_two, axis=0)
    grad_n_two = grad_h_two * norm_gain2
    grad_resid = own_rows(out_grad, zl).astype(F32) + factor_two * (
        grad_n_two - normed_two * jnp.mean(grad_n_two * normed_two, axis=-1, keepdims=True)
    )
    grad_branch = both_rows(grad_resid.astype(BF), zl)
    mine, theirs, d_attn, bias_term = attention_backward(
        side, grad_branch, h_one, attn_full, attended, qkv, probs, cosine, sine
    )

    grad_h_one = mine + hop(theirs, "zl", 1).astype(F32)
    my_normed = own_rows(normed_one, zl)
    gain_one_term = jnp.sum(grad_h_one * my_normed, axis=0)
    grad_n_one = grad_h_one * norm_gain1
    grad_tokens = grad_resid + own_rows(factor_one, zl) * (
        grad_n_one - my_normed * jnp.mean(grad_n_one * my_normed, axis=-1, keepdims=True)
    )
    grad_tokens = both_rows(grad_tokens.astype(BF), zl).astype(F32)

    d_attn = scatter_attn(d_attn, spot)
    d_query, d_key = d_attn[0, :, : HEADS * HD], d_attn[0, :, HEADS * HD :]
    d_value, d_outproj = d_attn[1, :, :HD], d_attn[1, :, HD:]
    vectors = jnp.concatenate([gain_one_term, gain_two_term, bias_term[0]]).reshape(32, 128)
    vectors = sum_vectors(vectors, spot).reshape(-1)
    gain_one, gain_two, d_qbias, d_kbias, d_vbias = jnp.split(
        vectors, [1536, 3072, 3072 + HEADS * HD, 3072 + ATT]
    )
    return (
        mixed_out,
        grad_tokens,
        gain_one,
        d_query,
        d_qbias,
        d_key,
        d_kbias,
        d_value,
        d_vbias,
        d_outproj.T,
        gain_two,
        d_gate,
        d_up,
        d_down.T,
    )


def solution(mesh):
    split = Mesh(mesh.devices.reshape(4, 4, 2, 2, 2), EVERY)
    return jax.shard_map(
        on_device,
        mesh=split,
        in_specs=(
            P(WIDE, None),
            P(WIDE, None),
            P(),
            P(WIDE, "zl"),
            P("zl"),
            P(WIDE, "zl"),
            P("zl"),
            P(WIDE, "zl"),
            P("zl"),
            P("zl", WIDE),
            P(),
            P(WIDE, "zl"),
            P(WIDE, "zl"),
            P("zl", WIDE),
            P(WIDE, None),
        ),
        out_specs=(
            P(WIDE, None),
            P(WIDE, None),
            P(),
            P(WIDE, "zl"),
            P("zl"),
            P(WIDE, "zl"),
            P("zl"),
            P(WIDE, "zl"),
            P("zl"),
            P("zl", WIDE),
            P(),
            P(WIDE, "zl"),
            P(WIDE, "zl"),
            P("zl", WIDE),
        ),
        check_vma=False,
    )
```

time: 699 us -> 389 us (0.56)
  the two profiles are of different devices: /device:TPU:8 before, /device:TPU:1 now
where the time goes in v2:
time: 389 us; the launch traced here: 381 us
  waiting for transfers between devices  132 us (34%)
  starting transfers between devices  99.9 us (26%)
  matrix products  55.3 us (14%)
  local copies, waits for them, and re-layouts  38.5 us (10%)
  other arithmetic  24.9 us (6%)
  between operations  15.7 us (4%)
  Pallas kernels  15.3 us (4%)
    ppermute x44, waiting for transfers between devices, hop(): lax.ppermute(value, axis, [(i, (i + step) % size) for i in range(size)])  81.5 us
    ppermute x44, starting transfers between devices, hop(): lax.ppermute(value, axis, [(i, (i + step) % size) for i in range(size)])  54.3 us
    ppermute x12, waiting for transfers between devices, zhop(): lax.ppermute(value, ('zh', 'zl'), [(i, (i + step) % 4) for i in range(4)])  29 us
    dot_general x2, matrix products, mm(): return jnp.dot(left, right, preferred_element_type=F32)  22.7 us
    ppermute x6, starting transfers between devices, quad_hop(): return lax.ppermute(value, ('zh', 'c'), [(i, i ^ flip) for i in range(4)])  18.6 us
    dot_general x2, matrix products, contract_cols(): lax.dot_general(left, right, (((1,), (1,)), ((), ())), preferred_element_...  17.8 us
    ppermute x12, starting transfers between devices, zhop(): lax.ppermute(value, ('zh', 'zl'), [(i, (i + step) % 4) for i in range(4)])  17.2 us
    ppermute x6, waiting for transfers between devices, trade(): block = lax.ppermute(block, ('zh', 'c'), [(i, i ^ k) for i in range(4)])  15.7 us
  transfers between devices with their start and end apart: 70, of which 33 were waited for; matrix products, arithmetic and copies ran while one was open for 17% of the time, Pallas kernels for 4%

profile of v2, /device:TPU:1, one launch (start us, length us, event | category | flops | bytes accessed | tf_op | source)
XLA Modules:
  0.0 381.3 jit_solution(10948719762975718590)
XLA Ops:
  11.4 3.7 collective-permute-start.23
  15.1 7.9 %collective-permute-done.22 = bf16[24,3456]{1,0:T(8,128)(2,1)S(1)} collective-permute-done((bf16[24,3456]{1,0:T(8,128)(2,1)S(1)}, bf16[24,3456]{1,0:T(8,128)(2,1)S(1)}, u32[]{:S(2)}, u32[]{:S(2)}) %collective-permute-start.22) | collective-permute-done | bytes 165920 | tf_op jit(solution)/shard_map/ppermute | solution.py:136
  25.1 2.9 collective-permute-start.2
  28.1 4.3 %collective-permute-done.1 = bf16[1,24,896]{2,1,0:T(8,128)(2,1)S(1)} collective-permute-done((bf16[1,24,896]{2,1,0:T(8,128)(2,1)S(1)}, bf16[1,24,896]{2,1,0:T(8,128)(2,1)S(1)}, u32[]{:S(2)}, u32[]{:S(2)}) %collective-permute-start.1) | collective-permute-done | bytes 43040 | tf_op jit(solution)/shard_map/ppermute | solution.py:57
  46.0 3.4 collective-permute-done.5
  58.2 3.7 collective-permute-done.6
  62.7 7.1 %collective-permute-done.7 = bf16[1,4,96,512]{3,2,1,0:T(8,128)(2,1)S(1)} collective-permute-done((bf16[1,4,96,512]{3,2,1,0:T(8,128)(2,1)S(1)}, bf16[1,4,96,512]{3,2,1,0:T(8,128)(2,1)S(1)}, u32[]{:S(2)}, u32[]{:S(2)}) %collective-permute-start.7) | collective-permute-done | bytes 393248 | tf_op jit(solution)/shard_map/ppermute | solution.py:35
  74.4 11.3 %collective-permute-start.15 = (bf16[1,1536,896]{2,1,0:T(8,128)(2,1)}, bf16[1,1536,896]{2,1,0:T(8,128)(2,1)}, u32[]{:S(2)}, u32[]{:S(2)}) collective-permute-start(bf16[1,1536,896]{2,1,0:T(8,128)(2,1)} %bitcast.13), channel_id=1, source_target_pairs={{0,2},{2,0},{1,3},{3,1},{4,6},{6,4},{5,7},{7,5},{8,10},{10,8},{9,1... | collective-permute-start | bytes 8257544 | tf_op jit(solution)/shard_map/ppermute | solution.py:35
  86.7 6.9 %collective-permute-start.31 = (bf16[128,1536]{1,0:T(8,128)(2,1)}, bf16[128,1536]{1,0:T(8,128)(2,1)}, u32[]{:S(2)}, u32[]{:S(2)}) collective-permute-start(bf16[128,1536]{1,0:T(8,128)(2,1)} %get-tuple-element.44), channel_id=1, source_target_pairs={{0,4},{1,5},{4,0},{5,1},{2,6},{3,7},{6,2},{7,3},{8,12},{9,13},{12,... | collective-permute-start | bytes 1179656 | tf_op jit(solution)/shard_map/ppermute | solution.py:39
  105.5 5.7 %shard_map.254 = (f32[128,1536]{1,0:T(8,128)S(1)}, bf16[128,1536]{1,0:T(8,128)(2,1)S(1)}, bf16[256,768]{1,0:T(8,128)(2,1)S(1)}, bf16[256,1024]{1,0:T(8,128)(2,1)S(1)}, f32[6,256,256]{2,1,0:T(8,128)S(1)}) custom-call(s32[1]{0:T(128)} %bitcast.side, bf16[256,1536]{1,0:T(8,128)(2,1)S(1)} %get-tuple-element.72.h, bf16[2,1536,896]{2,1,0:T(8,128)(2,1)} %copy-done.6, ...), custom_call_target="tpu_custom_call" | custom-call | flops 2200000000 | bytes 12000000 | tf_op jit(solution)/shard_map/pallas_call | solution.py:198
  114.7 6.4 %collective-permute-done.16 = bf16[128,1536]{1,0:T(8,128)(2,1)S(1)} collective-permute-done((bf16[128,1536]{1,0:T(8,128)(2,1)S(1)}, bf16[128,1536]{1,0:T(8,128)(2,1)S(1)}, u32[]{:S(2)}, u32[]{:S(2)}) %collective-permute-start.16) | collective-permute-done | bytes 393248 | tf_op jit(solution)/shard_map/ppermute | solution.py:35
  125.8 6.9 %collective-permute-done.19 = bf16[128,1536]{1,0:T(8,128)(2,1)S(1)} collective-permute-done((bf16[128,1536]{1,0:T(8,128)(2,1)S(1)}, bf16[128,1536]{1,0:T(8,128)(2,1)S(1)}, u32[]{:S(2)}, u32[]{:S(2)}) %collective-permute-start.19) | collective-permute-done | bytes 393248 | tf_op jit(solution)/shard_map/ppermute | solution.py:39
  132.7 9.1 %collective-permute-done.18 = bf16[128,1536]{1,0:T(8,128)(2,1)S(1)} collective-permute-done((bf16[128,1536]{1,0:T(8,128)(2,1)S(1)}, bf16[128,1536]{1,0:T(8,128)(2,1)S(1)}, u32[]{:S(2)}, u32[]{:S(2)}) %collective-permute-start.18) | collective-permute-done | bytes 393248 | tf_op jit(solution)/shard_map/ppermute | solution.py:39
  151.6 13.4 %fusion.2 = f32[1024,2304]{1,0:T(8,128)} fusion(bf16[1024,1536]{1,0:T(8,128)(2,1)} %constant_dynamic-update-slice_fusion, bf16[1536,3456]{1,0:T(8,128)(2,1)} %all-gather.2.cloned.1.call-done), kind=kOutput, calls=%fused_computation.5 | convolution fusion | flops 7247757312 | bytes 19660800 | tf_op jit(solution)/shard_map/dot_general | solution.py:22
  165.0 9.3 %multiply_convert_fusion.1 = (bf16[1024,1152]{1,0:T(8,128)(2,1)S(1)}, bf16[1024,1152]{1,0:T(8,128)(2,1)S(1)}, bf16[1024,1152]{1,0:T(8,128)(2,1)S(1)}) fusion(f32[1024,2304]{1,0:T(8,128)} %fusion.2, bf16[1024,1536]{1,0:T(8,128)(2,1)S(1)} %copy-done.17, bf16[1536,3456]{1,0:T(8,128)(2,1)} %all-gather.2.cloned.1.call-done), kind=kOutput, calls=%fused_computation.11 | convolution fusion | flops 3641573376 | bytes 23199744 | tf_op jit(solution)/shard_map/dot_general | solution.py:22
  174.3 4.6 %convolution_convert_fusion.1 = bf16[1536,1152]{1,0:T(8,128)(2,1)S(1)} fusion(bf16[1024,1536]{1,0:T(8,128)(2,1)S(1)} %copy-done.17, bf16[1024,1152]{1,0:T(8,128)(2,1)S(1)} %get-tuple-element.55), kind=kOutput, calls=%fused_computation.2 | convolution fusion | flops 3625648128 | bytes 9043968 | tf_op jit(solution)/shard_map/dot_general | solution.py:26
  178.9 10.2 %convolution_convert_fusion = bf16[1536,2304]{1,0:T(8,128)(2,1)S(1)} fusion(bf16[1024,1536]{1,0:T(8,128)(2,1)} %constant_dynamic-update-slice_fusion, bf16[1024,1152]{1,0:T(8,128)(2,1)S(1)} %get-tuple-element.54, bf16[1024,1152]{1,0:T(8,128)(2,1)S(1)} %get-tuple-element.53), kind=kOutput, calls=%fused_computation | convolution fusion | flops 7260733440 | bytes 14942208 | tf_op jit(solution)/shard_map/dot_general | solution.py:26
  189.1 4.9 %pad_maximum_fusion = bf16[1536,3456]{1,0:T(8,128)(2,1)} fusion(bf16[1536,1152]{1,0:T(8,128)(2,1)S(1)} %convolution_convert_fusion.1, bf16[1536,2304]{1,0:T(8,128)(2,1)S(1)} %convolution_convert_fusion), kind=kLoop, calls=%fused_computation.1 | loop fusion | flops 21233664 | bytes 21233664 | tf_op jit(solution)/shard_map/concatenate | solution.py:353
  194.0 11.4 %fusion = f32[1024,1536]{1,0:T(8,128)S(1)} fusion(bf16[1536,3456]{1,0:T(8,128)(2,1)} %all-gather.2.cloned.1.call-done, bf16[1024,1152]{1,0:T(8,128)(2,1)} %copy-done.34, bf16[1024,1152]{1,0:T(8,128)(2,1)} %copy-done.33), kind=kOutput, calls=%fused_computation.3 | convolution fusion | flops 7257194496 | bytes 18087936 | tf_op jit(solution)/shard_map/dot_general | solution.py:30
  205.7 3.4 collective-permute-done.33
  212.7 6.5 %fusion.8 = f32[1024,1536]{1,0:T(8,128)S(1)} fusion(bf16[1024,1152]{1,0:T(8,128)(2,1)S(1)} %copy-done.36, bf16[1536,3456]{1,0:T(8,128)(2,1)} %all-gather.2.cloned.1.call-done), kind=kOutput, calls=%fused_computation.21 | convolution fusion | flops 3623878656 | bytes 12189696 | tf_op jit(solution)/shard_map/dot_general | solution.py:30
  223.6 9.3 %collective-permute-done.35 = bf16[128,1536]{1,0:T(8,128)(2,1)S(1)} collective-permute-done((bf16[128,1536]{1,0:T(8,128)(2,1)S(1)}, bf16[128,1536]{1,0:T(8,128)(2,1)S(1)}, u32[]{:S(2)}, u32[]{:S(2)}) %collective-permute-start.35) | collective-permute-done | bytes 393248 | tf_op jit(solution)/shard_map/ppermute | solution.py:39
  237.7 9.2 %collective-permute-done.37 = bf16[128,1536]{1,0:T(8,128)(2,1)} collective-permute-done((bf16[128,1536]{1,0:T(8,128)(2,1)}, bf16[128,1536]{1,0:T(8,128)(2,1)}, u32[]{:S(2)}, u32[]{:S(2)}) %collective-permute-start.37) | collective-permute-done | bytes 393248 | tf_op jit(solution)/shard_map/ppermute | solution.py:35
  248.2 9.6 %shard_map.255 = (f32[128,1536]{1,0:T(8,128)S(1)}, bf16[128,1536]{1,0:T(8,128)(2,1)S(1)}, bf16[2,1536,896]{2,1,0:T(8,128)(2,1)}, f32[1,1024]{1,0:T(1,128)S(1)}) custom-call(s32[1]{0:T(128)} %bitcast.side, bf16[256,1536]{1,0:T(8,128)(2,1)S(1)} %bitcast.204, bf16[256,1536]{1,0:T(8,128)(2,1)S(1)} %get-tuple-element.72.h, bf16[2,1536,896]{2,1,0:T(8,128)(2,1)} %copy-done.6, ...), custom_call_target="tpu_custom_call" | custom-call | flops 4300000256 | bytes 20000000 | tf_op jit(solution)/shard_map/pallas_call | solution.py:251
  260.6 6.7 %collective-permute-done.38 = bf16[128,1536]{1,0:T(8,128)(2,1)S(1)} collective-permute-done((bf16[128,1536]{1,0:T(8,128)(2,1)S(1)}, bf16[128,1536]{1,0:T(8,128)(2,1)S(1)}, u32[]{:S(2)}, u32[]{:S(2)}) %collective-permute-start.38) | collective-permute-done | bytes 393248 | tf_op jit(solution)/shard_map/ppermute | solution.py:35
  273.2 3.5 collective-permute-done.41
  279.6 4.1 %collective-permute-done.43 = f32[32,128]{1,0:T(8,128)S(1)} collective-permute-done((f32[32,128]{1,0:T(8,128)S(1)}, f32[32,128]{1,0:T(8,128)S(1)}, u32[]{:S(2)}, u32[]{:S(2)}) %collective-permute-start.43) | collective-permute-done | bytes 16416 | tf_op jit(solution)/shard_map/ppermute | solution.py:35
  283.9 4.1 %collective-permute-done.44 = f32[32,128]{1,0:T(8,128)S(1)} collective-permute-done((f32[32,128]{1,0:T(8,128)S(1)}, f32[32,128]{1,0:T(8,128)S(1)}, u32[]{:S(2)}, u32[]{:S(2)}) %collective-permute-start.44) | collective-permute-done | bytes 16416 | tf_op jit(solution)/shard_map/ppermute | solution.py:35
  290.8 4.1 %collective-permute-done.46 = f32[32,128]{1,0:T(8,128)S(1)} collective-permute-done((f32[32,128]{1,0:T(8,128)S(1)}, f32[32,128]{1,0:T(8,128)S(1)}, u32[]{:S(2)}, u32[]{:S(2)}) %collective-permute-start.46) | collective-permute-done | bytes 16416 | tf_op jit(solution)/shard_map/ppermute | solution.py:35
  302.9 8.6 %collective-permute-done.48 = f32[24,128]{1,0:T(8,128)S(1)} collective-permute-done((f32[24,128]{1,0:T(8,128)S(1)}, f32[24,128]{1,0:T(8,128)S(1)}, u32[]{:S(2)}, u32[]{:S(2)}) %collective-permute-start.48) | collective-permute-done | bytes 12320 | tf_op jit(solution)/shard_map/ppermute | solution.py:35
  339.5 13.1 %collective-permute-start.64 = (bf16[24,896]{1,0:T(8,128)(2,1)S(1)}, bf16[24,896]{1,0:T(8,128)(2,1)S(1)}, u32[]{:S(2)}, u32[]{:S(2)}) collective-permute-start(bf16[24,896]{1,0:T(8,128)(2,1)S(1)} %get-tuple-element.95), channel_id=1, source_target_pairs={{0,6},{2,4},{4,2},{6,0},{1,7},{3,5},{5,3},{7,1},{8,14},{10,12},{12... | collective-permute-start | bytes 129032 | tf_op jit(solution)/shard_map/ppermute | solution.py:57
  363.1 7.7 %collective-permute-done.66 = bf16[24,3456]{1,0:T(8,128)(2,1)S(1)} collective-permute-done((bf16[24,3456]{1,0:T(8,128)(2,1)S(1)}, bf16[24,3456]{1,0:T(8,128)(2,1)S(1)}, u32[]{:S(2)}, u32[]{:S(2)}) %collective-permute-start.66) | collective-permute-done | bytes 165920 | tf_op jit(solution)/shard_map/ppermute | solution.py:136
  (335 shorter events, 142.7 us)
Async XLA Ops:
  7.2 144.4 %all-gather.2.cloned.1.call-start = ((), (), s32[]{:S(2)}) async-start(), calls=%async_computation.1 | async-start | bytes 11280384 | tf_op jit(solution)/shard_map/all_gather | solution.py:318
  11.4 11.7 %collective-permute-start.23 = (bf16[24,3456]{1,0:T(8,128)(2,1)S(1)}, bf16[24,3456]{1,0:T(8,128)(2,1)S(1)}, u32[]{:S(2)}, u32[]{:S(2)}) collective-permute-start(bf16[24,3456]{1,0:T(8,128)(2,1)S(1)} %get-tuple-element.85), channel_id=1, source_target_pairs={{0,6},{2,4},{4,2},{6,0},{1,7},{3,5},{5,3},{7,1},{8,14},{10,12},{12... | collective-permute-start | bytes 497672 | tf_op jit(solution)/shard_map/ppermute | solution.py:136
  24.0 332.7 %reduce-scatter.2.cloned.1.call-start = ((), (), s32[]{:S(2)}) async-start(), calls=%async_computation.2 | async-start | bytes 11280384 | tf_op jit(solution)/shard_map/reduce_scatter | solution.py:358
  32.4 18.8 %collective-permute-start.10 = (bf16[1,96,384]{2,1,0:T(8,128)(2,1)S(1)}, bf16[1,96,384]{2,1,0:T(8,128)(2,1)S(1)}, u32[]{:S(2)}, u32[]{:S(2)}) collective-permute-start(bf16[1,96,384]{2,1,0:T(8,128)(2,1)S(1)} %slice.166), channel_id=1, source_target_pairs={{0,96},{32,0},{64,32},{96,64},{1,97},{33,1},{65,33},{97,65},{2,98}... | collective-permute-start | bytes 221192 | tf_op jit(solution)/shard_map/ppermute | solution.py:35
  35.2 18.5 %collective-permute-start.11 = (bf16[1,96,384]{2,1,0:T(8,128)(2,1)S(1)}, bf16[1,96,384]{2,1,0:T(8,128)(2,1)S(1)}, u32[]{:S(2)}, u32[]{:S(2)}) collective-permute-start(bf16[1,96,384]{2,1,0:T(8,128)(2,1)S(1)} %slice.166), channel_id=1, source_target_pairs={{0,64},{32,96},{64,0},{96,32},{1,65},{33,97},{65,1},{97,33},{2,66}... | collective-permute-start | bytes 221192 | tf_op jit(solution)/shard_map/ppermute | solution.py:35
  49.4 12.5 %collective-permute-start.6 = (bf16[1,4,96,512]{3,2,1,0:T(8,128)(2,1)S(1)}, bf16[1,4,96,512]{3,2,1,0:T(8,128)(2,1)S(1)}, u32[]{:S(2)}, u32[]{:S(2)}) collective-permute-start(bf16[1,4,96,512]{3,2,1,0:T(8,128)(2,1)S(1)} %bitcast_dynamic-update-slice_fusion.6), channel_id=1, source_target_pairs={{0,32},{32,64},{64,96},{96,0},{1,33},{33,65},{65,97},{97,1},{2,34}... | collective-permute-start | bytes 1179656 | tf_op jit(solution)/shard_map/ppermute | solution.py:35
  51.2 19.3 %collective-permute-start.8 = (bf16[1,4,96,512]{3,2,1,0:T(8,128)(2,1)S(1)}, bf16[1,4,96,512]{3,2,1,0:T(8,128)(2,1)S(1)}, u32[]{:S(2)}, u32[]{:S(2)}) collective-permute-start(bf16[1,4,96,512]{3,2,1,0:T(8,128)(2,1)S(1)} %bitcast_dynamic-update-slice_fusion.6), channel_id=1, source_target_pairs={{0,64},{32,96},{64,0},{96,32},{1,65},{33,97},{65,1},{97,33},{2,66}... | collective-permute-start | bytes 1179656 | tf_op jit(solution)/shard_map/ppermute | solution.py:35
  52.0 17.8 %collective-permute-start.7 = (bf16[1,4,96,512]{3,2,1,0:T(8,128)(2,1)S(1)}, bf16[1,4,96,512]{3,2,1,0:T(8,128)(2,1)S(1)}, u32[]{:S(2)}, u32[]{:S(2)}) collective-permute-start(bf16[1,4,96,512]{3,2,1,0:T(8,128)(2,1)S(1)} %bitcast_dynamic-update-slice_fusion.6), channel_id=1, source_target_pairs={{0,96},{32,0},{64,32},{96,64},{1,97},{33,1},{65,33},{97,65},{2,98}... | collective-permute-start | bytes 1179656 | tf_op jit(solution)/shard_map/ppermute | solution.py:35
  53.7 19.9 %collective-permute-start.14 = (bf16[4,1,96,384]{3,2,1,0:T(8,128)(2,1)S(1)}, bf16[4,1,96,384]{3,2,1,0:T(8,128)(2,1)S(1)}, u32[]{:S(2)}, u32[]{:S(2)}) collective-permute-start(bf16[4,1,96,384]{3,2,1,0:T(8,128)(2,1)S(1)} %bitcast_dynamic-update-slice_fusion.10), channel_id=1, source_target_pairs={{0,16},{8,24},{16,0},{24,8},{1,17},{9,25},{17,1},{25,9},{2,18},{10... | collective-permute-start | bytes 884744 | tf_op jit(solution)/shard_map/ppermute | solution.py:35
  54.6 18.3 %collective-permute-start.13 = (bf16[4,1,96,384]{3,2,1,0:T(8,128)(2,1)S(1)}, bf16[4,1,96,384]{3,2,1,0:T(8,128)(2,1)S(1)}, u32[]{:S(2)}, u32[]{:S(2)}) collective-permute-start(bf16[4,1,96,384]{3,2,1,0:T(8,128)(2,1)S(1)} %bitcast_dynamic-update-slice_fusion.10), channel_id=1, source_target_pairs={{0,24},{8,0},{16,8},{24,16},{1,25},{9,1},{17,9},{25,17},{2,26},{10... | collective-permute-start | bytes 884744 | tf_op jit(solution)/shard_map/ppermute | solution.py:35
  74.4 26.4 %collective-permute-start.15 = (bf16[1,1536,896]{2,1,0:T(8,128)(2,1)}, bf16[1,1536,896]{2,1,0:T(8,128)(2,1)}, u32[]{:S(2)}, u32[]{:S(2)}) collective-permute-start(bf16[1,1536,896]{2,1,0:T(8,128)(2,1)} %bitcast.13), channel_id=1, source_target_pairs={{0,2},{2,0},{1,3},{3,1},{4,6},{6,4},{5,7},{7,5},{8,10},{10,8},{9,1... | collective-permute-start | bytes 8257544 | tf_op jit(solution)/shard_map/ppermute | solution.py:35
  86.7 25.3 %collective-permute-start.31 = (bf16[128,1536]{1,0:T(8,128)(2,1)}, bf16[128,1536]{1,0:T(8,128)(2,1)}, u32[]{:S(2)}, u32[]{:S(2)}) collective-permute-start(bf16[128,1536]{1,0:T(8,128)(2,1)} %get-tuple-element.44), channel_id=1, source_target_pairs={{0,4},{1,5},{4,0},{5,1},{2,6},{3,7},{6,2},{7,3},{8,12},{9,13},{12,... | collective-permute-start | bytes 1179656 | tf_op jit(solution)/shard_map/ppermute | solution.py:39
  93.6 18.7 %collective-permute-start.30 = (bf16[128,1536]{1,0:T(8,128)(2,1)}, bf16[128,1536]{1,0:T(8,128)(2,1)}, u32[]{:S(2)}, u32[]{:S(2)}) collective-permute-start(bf16[128,1536]{1,0:T(8,128)(2,1)} %get-tuple-element.44), channel_id=1, source_target_pairs={{0,5},{1,0},{4,1},{5,4},{2,7},{3,2},{6,3},{7,6},{8,13},{9,8},{12,9... | collective-permute-start | bytes 1179656 | tf_op jit(solution)/shard_map/ppermute | solution.py:39
  94.2 18.1 %collective-permute-start.29 = (bf16[128,1536]{1,0:T(8,128)(2,1)}, bf16[128,1536]{1,0:T(8,128)(2,1)}, u32[]{:S(2)}, u32[]{:S(2)}) collective-permute-start(bf16[128,1536]{1,0:T(8,128)(2,1)} %get-tuple-element.44), channel_id=1, source_target_pairs={{0,1},{1,4},{4,5},{5,0},{2,3},{3,6},{6,7},{7,2},{8,9},{9,12},{12,1... | collective-permute-start | bytes 1179656 | tf_op jit(solution)/shard_map/ppermute | solution.py:39
  113.8 33.7 %collective-permute-start.32 = (bf16[512,1536]{1,0:T(8,128)(2,1)S(1)}, bf16[512,1536]{1,0:T(8,128)(2,1)S(1)}, u32[]{:S(2)}, u32[]{:S(2)}) collective-permute-start(bf16[512,1536]{1,0:T(8,128)(2,1)S(1)} %pad_maximum_fusion.5), channel_id=1, source_target_pairs={{0,2},{2,0},{1,3},{3,1},{4,6},{6,4},{5,7},{7,5},{8,10},{10,8},{9,1... | collective-permute-start | bytes 4718600 | tf_op jit(solution)/shard_map/ppermute | solution.py:35
  124.3 17.5 %collective-permute-start.18 = (bf16[128,1536]{1,0:T(8,128)(2,1)S(1)}, bf16[128,1536]{1,0:T(8,128)(2,1)S(1)}, u32[]{:S(2)}, u32[]{:S(2)}) collective-permute-start(bf16[128,1536]{1,0:T(8,128)(2,1)S(1)} %get-tuple-element.48), channel_id=1, source_target_pairs={{0,5},{1,0},{4,1},{5,4},{2,7},{3,2},{6,3},{7,6},{8,13},{9,8},{12,9... | collective-permute-start | bytes 1179656 | tf_op jit(solution)/shard_map/ppermute | solution.py:39
  125.5 17.8 %collective-permute-start.17 = (bf16[128,1536]{1,0:T(8,128)(2,1)S(1)}, bf16[128,1536]{1,0:T(8,128)(2,1)S(1)}, u32[]{:S(2)}, u32[]{:S(2)}) collective-permute-start(bf16[128,1536]{1,0:T(8,128)(2,1)S(1)} %get-tuple-element.48), channel_id=1, source_target_pairs={{0,1},{1,4},{4,5},{5,0},{2,3},{3,6},{6,7},{7,2},{8,9},{9,12},{12,1... | collective-permute-start | bytes 1179656 | tf_op jit(solution)/shard_map/ppermute | solution.py:39
  209.8 11.9 %collective-permute-start.34 = (bf16[128,1536]{1,0:T(8,128)(2,1)S(1)}, bf16[128,1536]{1,0:T(8,128)(2,1)S(1)}, u32[]{:S(2)}, u32[]{:S(2)}) collective-permute-start(bf16[128,1536]{1,0:T(8,128)(2,1)S(1)} %get-tuple-element.59), channel_id=1, source_target_pairs={{0,5},{1,0},{4,1},{5,4},{2,7},{3,2},{6,3},{7,6},{8,13},{9,8},{12,9... | collective-permute-start | bytes 1179656 | tf_op jit(solution)/shard_map/ppermute | solution.py:39
  211.8 11.8 %collective-permute-start.36 = (bf16[128,1536]{1,0:T(8,128)(2,1)S(1)}, bf16[128,1536]{1,0:T(8,128)(2,1)S(1)}, u32[]{:S(2)}, u32[]{:S(2)}) collective-permute-start(bf16[128,1536]{1,0:T(8,128)(2,1)S(1)} %get-tuple-element.60), channel_id=1, source_target_pairs={{0,4},{1,5},{4,0},{5,1},{2,6},{3,7},{6,2},{7,3},{8,12},{9,13},{12,... | collective-permute-start | bytes 1179656 | tf_op jit(solution)/shard_map/ppermute | solution.py:39
  212.4 20.5 %collective-permute-start.35 = (bf16[128,1536]{1,0:T(8,128)(2,1)S(1)}, bf16[128,1536]{1,0:T(8,128)(2,1)S(1)}, u32[]{:S(2)}, u32[]{:S(2)}) collective-permute-start(bf16[128,1536]{1,0:T(8,128)(2,1)S(1)} %get-tuple-element.61), channel_id=1, source_target_pairs={{0,1},{1,4},{4,5},{5,0},{2,3},{3,6},{6,7},{7,2},{8,9},{9,12},{12,1... | collective-permute-start | bytes 1179656 | tf_op jit(solution)/shard_map/ppermute | solution.py:39
  220.5 37.7 %collective-permute-start.24 = (bf16[512,1536]{1,0:T(8,128)(2,1)}, bf16[512,1536]{1,0:T(8,128)(2,1)}, u32[]{:S(2)}, u32[]{:S(2)}) collective-permute-start(bf16[512,1536]{1,0:T(8,128)(2,1)} %slice.264), channel_id=1, source_target_pairs={{0,2},{2,0},{1,3},{3,1},{4,6},{6,4},{5,7},{7,5},{8,10},{10,8},{9,1... | collective-permute-start | bytes 4718600 | tf_op jit(solution)/shard_map/ppermute | solution.py:35
  270.0 27.3 %collective-permute-start.25 = (bf16[128,1536]{1,0:T(8,128)(2,1)S(1)}, bf16[128,1536]{1,0:T(8,128)(2,1)S(1)}, u32[]{:S(2)}, u32[]{:S(2)}) collective-permute-start(bf16[128,1536]{1,0:T(8,128)(2,1)S(1)} %get-tuple-element.62), channel_id=1, source_target_pairs={{0,5},{1,0},{4,1},{5,4},{2,7},{3,2},{6,3},{7,6},{8,13},{9,8},{12,9... | collective-permute-start | bytes 1179656 | tf_op jit(solution)/shard_map/ppermute | solution.py:39
  270.0 27.2 %collective-permute-start.27 = (bf16[128,1536]{1,0:T(8,128)(2,1)S(1)}, bf16[128,1536]{1,0:T(8,128)(2,1)S(1)}, u32[]{:S(2)}, u32[]{:S(2)}) collective-permute-start(bf16[128,1536]{1,0:T(8,128)(2,1)S(1)} %get-tuple-element.63), channel_id=1, source_target_pairs={{0,4},{1,5},{4,0},{5,1},{2,6},{3,7},{6,2},{7,3},{8,12},{9,13},{12,... | collective-permute-start | bytes 1179656 | tf_op jit(solution)/shard_map/ppermute | solution.py:39
  272.2 25.1 %collective-permute-start.26 = (bf16[128,1536]{1,0:T(8,128)(2,1)S(1)}, bf16[128,1536]{1,0:T(8,128)(2,1)S(1)}, u32[]{:S(2)}, u32[]{:S(2)}) collective-permute-start(bf16[128,1536]{1,0:T(8,128)(2,1)S(1)} %get-tuple-element.64), channel_id=1, source_target_pairs={{0,1},{1,4},{4,5},{5,0},{2,3},{3,6},{6,7},{7,2},{8,9},{9,12},{12,1... | collective-permute-start | bytes 1179656 | tf_op jit(solution)/shard_map/ppermute | solution.py:39
  272.6 39.6 %collective-permute-start.49 = (bf16[1536,896]{1,0:T(8,128)(2,1)S(1)}, bf16[1536,896]{1,0:T(8,128)(2,1)S(1)}, u32[]{:S(2)}, u32[]{:S(2)}) collective-permute-start(bf16[1536,896]{1,0:T(8,128)(2,1)S(1)} %dynamic-slice_bitcast_fusion), channel_id=1, source_target_pairs={{0,2},{2,0},{1,3},{3,1},{4,6},{6,4},{5,7},{7,5},{8,10},{10,8},{9,1... | collective-permute-start | bytes 8257544 | tf_op jit(solution)/shard_map/ppermute | solution.py:35
  299.0 13.1 %collective-permute-start.39 = (bf16[128,1536]{1,0:T(8,128)(2,1)S(1)}, bf16[128,1536]{1,0:T(8,128)(2,1)S(1)}, u32[]{:S(2)}, u32[]{:S(2)}) collective-permute-start(bf16[128,1536]{1,0:T(8,128)(2,1)S(1)} %get-tuple-element.75), channel_id=1, source_target_pairs={{0,1},{1,0},{2,3},{3,2},{4,5},{5,4},{6,7},{7,6},{8,9},{9,8},{10,11... | collective-permute-start | bytes 1179656 | tf_op jit(solution)/shard_map/ppermute | solution.py:35
  300.0 18.0 %collective-permute-start.28 = (bf16[128,1536]{1,0:T(8,128)(2,1)S(1)}, bf16[128,1536]{1,0:T(8,128)(2,1)S(1)}, u32[]{:S(2)}, u32[]{:S(2)}) collective-permute-start(bf16[128,1536]{1,0:T(8,128)(2,1)S(1)} %get-tuple-element.76), channel_id=1, source_target_pairs={{0,1},{1,0},{2,3},{3,2},{4,5},{5,4},{6,7},{7,6},{8,9},{9,8},{10,11... | collective-permute-start | bytes 1179656 | tf_op jit(solution)/shard_map/ppermute | solution.py:35
  300.6 10.9 %collective-permute-start.48 = (f32[24,128]{1,0:T(8,128)S(1)}, f32[24,128]{1,0:T(8,128)S(1)}, u32[]{:S(2)}, u32[]{:S(2)}) collective-permute-start(f32[24,128]{1,0:T(8,128)S(1)} %slice.191), channel_id=1, source_target_pairs={{0,1},{1,0},{2,3},{3,2},{4,5},{5,4},{6,7},{7,6},{8,9},{9,8},{10,11... | collective-permute-start | bytes 36872 | tf_op jit(solution)/shard_map/ppermute | solution.py:35
  317.8 11.0 %collective-permute-start.50 = (bf16[4,96,512]{2,1,0:T(8,128)(2,1)S(1)}, bf16[4,96,512]{2,1,0:T(8,128)(2,1)S(1)}, u32[]{:S(2)}, u32[]{:S(2)}) collective-permute-start(bf16[4,96,512]{2,1,0:T(8,128)(2,1)S(1)} %get-tuple-element.56), channel_id=1, source_target_pairs={{0,32},{32,64},{64,96},{96,0},{1,33},{33,65},{65,97},{97,1},{2,34}... | collective-permute-start | bytes 1179656 | tf_op jit(solution)/shard_map/ppermute | solution.py:35
  317.9 12.3 %collective-permute-start.52 = (bf16[4,96,512]{2,1,0:T(8,128)(2,1)S(1)}, bf16[4,96,512]{2,1,0:T(8,128)(2,1)S(1)}, u32[]{:S(2)}, u32[]{:S(2)}) collective-permute-start(bf16[4,96,512]{2,1,0:T(8,128)(2,1)S(1)} %get-tuple-element.57), channel_id=1, source_target_pairs={{0,64},{32,96},{64,0},{96,32},{1,65},{33,97},{65,1},{97,33},{2,66}... | collective-permute-start | bytes 1179656 | tf_op jit(solution)/shard_map/ppermute | solution.py:35
  337.8 15.8 %collective-permute-start.62 = (bf16[24,896]{1,0:T(8,128)(2,1)S(1)}, bf16[24,896]{1,0:T(8,128)(2,1)S(1)}, u32[]{:S(2)}, u32[]{:S(2)}) collective-permute-start(bf16[24,896]{1,0:T(8,128)(2,1)S(1)} %get-tuple-element.94), channel_id=1, source_target_pairs={{0,4},{2,6},{4,0},{6,2},{1,5},{3,7},{5,1},{7,3},{8,12},{10,14},{12... | collective-permute-start | bytes 129032 | tf_op jit(solution)/shard_map/ppermute | solution.py:57
  339.5 15.3 %collective-permute-start.64 = (bf16[24,896]{1,0:T(8,128)(2,1)S(1)}, bf16[24,896]{1,0:T(8,128)(2,1)S(1)}, u32[]{:S(2)}, u32[]{:S(2)}) collective-permute-start(bf16[24,896]{1,0:T(8,128)(2,1)S(1)} %get-tuple-element.95), channel_id=1, source_target_pairs={{0,6},{2,4},{4,2},{6,0},{1,7},{3,5},{5,3},{7,1},{8,14},{10,12},{12... | collective-permute-start | bytes 129032 | tf_op jit(solution)/shard_map/ppermute | solution.py:57
  (79 other events, 945.3 us)
Sparse Core Ops, SparseCore 0:
  24.2 93.4 all-gather.1
  194.1 84.4 reduce-scatter.1
